TPU v7x, 256 devices: a whole 4x4x8 slice. The times are simulated.
256 devices in a mesh: wall: 8 (over y, core), span: 4 (over x), stream: 8 (over z).
Axes of the slice: x: 4, y: 4, z: 8, core: 2. Of those that a mesh axis runs over, the one named last changes fastest.
Arguments:
- velocity: float32 [3, 1536, 128, 512], P(None, 'wall', 'stream', 'span'), may hold values from -6 to 6
- viscosity: float32 [1536], replicated, may hold values from 82944 to 165888
Outputs:
- predictor: float32 [3, 1536, 128, 512], P(None, 'wall', 'stream', 'span')
- velocity_new: float32 [3, 1536, 128, 512], P(None, 'wall', 'stream', 'span')
All inputs are finite; a program needn't handle non-finite values.
Results may differ from a plain program's by a relative error of at most 0.00055.
Values sent between devices are 32-bit elements; how exact they have to be, the bound alone decides.
No kernel may reach another device: no remote copies, remote signals or barrier semaphores. Data moves between devices by JAX's collectives and lax.ppermute only.
A program may use at most 192 MiB of HBM per device.

v0:
```python
import jax
import jax.numpy as jnp
from jax import lax
from jax.sharding import PartitionSpec as P

step_size = 0.5


def extended(block, sides, width, periodic):
    for axis, dim in sides:
        count = lax.axis_size(axis)
        forward = [(i, i + 1) for i in range(count - 1)]
        if periodic:
            forward.append((count - 1, 0))
        backward = [(target, source) for source, target in forward]
        low = lax.ppermute(
            lax.slice_in_dim(block, block.shape[dim] - width, None, axis=dim), axis, forward
        )
        high = lax.ppermute(lax.slice_in_dim(block, 0, width, axis=dim), axis, backward)
        block = jnp.concatenate([low, block, high], axis=dim)
    return block


def passed_along(value, axis, steps):
    count = lax.axis_size(axis)
    leading, last = (max(0, -steps), min(count, count - steps))
    return lax.ppermute(value, axis, [(source, source + steps) for source in range(leading, last)])


def sixth_order_stencil(padded, along_axis, length):

    def moved(offset):
        return lax.slice_in_dim(padded, 3 + offset, 3 + offset + length, axis=along_axis)

    return (
        45.0 * (moved(1) - moved(-1)) - 9.0 * (moved(2) - moved(-2)) + (moved(3) - moved(-3))
    ) / 60.0


def unrolled_solve(lower_coef, center_coef, upper_coefficient, right_side, along_axis):
    length = right_side.shape[along_axis]
    primes = []
    values = []
    for position in range(length):
        rhs_piece = lax.index_in_dim(right_side, position, along_axis, keepdims=False)
        if position == 0:
            pivot_value = center_coef[0]
            value_now = rhs_piece / pivot_value
        else:
            pivot_value = center_coef[position] - lower_coef[position] * primes[-1]
            value_now = (rhs_piece - lower_coef[position] * values[-1]) / pivot_value
        primes.append(upper_coefficient[position] / pivot_value)
        values.append(value_now)
    solved = [values[-1]]
    for position in range(length - 2, -1, -1):
        solved.insert(0, values[position] - primes[position] * solved[0])
    return jnp.stack(solved, axis=along_axis)


def line_solve(field, lower_coef, center_coef, upper_coefficient):
    tail_shape = field.shape[1:]

    def forward(state_now, inputs):
        prime_prev, value_prev = state_now
        lower_now, center_now, upper_now, rhs_now = inputs
        pivot_value = center_now - lower_now * prime_prev
        prime_next = upper_now / pivot_value
        value_next = (rhs_now - lower_now * value_prev) / pivot_value
        return ((prime_next, value_next), (prime_next, value_next))

    initial = (jnp.zeros((), jnp.float32), jnp.zeros(tail_shape, jnp.float32))
    closing_state, outputs = lax.scan(
        forward, initial, (lower_coef, center_coef, upper_coefficient, field)
    )

    def backward(later_value, inputs):
        prime_now, value_now = inputs
        solved = value_now - prime_now * later_value
        return (solved, solved)

    final_value, solved_all = lax.scan(
        backward, jnp.zeros(tail_shape, jnp.float32), outputs, reverse=True
    )
    return solved_all


def line_factors(viscosity, row_groups, depth_rows):
    inner_rows = depth_rows - 1
    face_high = jnp.concatenate([viscosity[1:], viscosity[-1:]])
    low_table = viscosity.reshape(row_groups, depth_rows)
    high_table = face_high.reshape(row_groups, depth_rows)
    center_table = 1.0 + low_table + high_table
    lower_coef = -low_table[:, :inner_rows].T
    upper_coefficient = -high_table[:, :inner_rows].T
    center_coef = center_table[:, :inner_rows].T
    first_flag = (jnp.arange(inner_rows) == 0).astype(jnp.float32)[:, None]
    last_flag = (jnp.arange(inner_rows) == inner_rows - 1).astype(jnp.float32)[:, None]
    from_below = unrolled_solve(
        lower_coef, center_coef, upper_coefficient, first_flag * low_table[:, 0][None, :], 0
    )
    from_above = unrolled_solve(
        lower_coef, center_coef, upper_coefficient, last_flag * low_table[:, inner_rows][None, :], 0
    )
    face_last = low_table[:, inner_rows]
    high_last = high_table[:, inner_rows]
    has_next = (jnp.arange(row_groups) < row_groups - 1).astype(jnp.float32)
    has_prev = (jnp.arange(row_groups) > 0).astype(jnp.float32)
    below_next = jnp.roll(from_below[0], -1)
    above_next = jnp.roll(from_above[0], -1)
    small_lower = -has_prev * face_last * from_below[inner_rows - 1]
    small_center = (
        center_table[:, inner_rows]
        - face_last * from_above[inner_rows - 1]
        - has_next * high_last * below_next
    )
    small_upper = -has_next * high_last * above_next

    def pivot_step(prime_prev, inputs):
        lower_now, center_now, upper_now = inputs
        pivot_value = center_now - lower_now * prime_prev
        return (upper_now / pivot_value, pivot_value)

    final_prime, pivots = lax.scan(
        pivot_step, jnp.zeros((), jnp.float32), (small_lower, small_center, small_upper)
    )
    pivots_prev = jnp.concatenate([jnp.ones((1,), jnp.float32), pivots[:-1]])
    return (
        lower_coef,
        center_coef,
        upper_coefficient,
        from_below,
        from_above,
        face_last,
        high_last,
        small_lower,
        small_center,
        small_upper,
        pivots,
        small_lower / pivots_prev,
    )


def on_device(velocity, viscosity):
    row_groups = lax.axis_size("wall")
    place = lax.axis_index("wall")
    depth_rows = velocity.shape[1]
    inner_rows = depth_rows - 1
    cells_x = velocity.shape[2]
    cells_z = velocity.shape[3]
    padded = extended(velocity, (("span", 3), ("stream", 2)), 3, True)
    walled = extended(velocity, (("wall", 1),), 1, False)
    slope_x = sixth_order_stencil(padded[:, :, :, 3 : 3 + cells_z], 2, cells_x)
    slope_z = sixth_order_stencil(padded[:, :, 3 : 3 + cells_x, :], 3, cells_z)
    slope_y = (walled[:, 2:] - walled[:, :-2]) * 0.5
    advect = velocity[0] * slope_x + velocity[1] * slope_y + velocity[2] * slope_z
    predictor = velocity - step_size * advect
    (
        lower_coef,
        center_coef,
        upper_coefficient,
        from_below,
        from_above,
        face_last,
        high_last,
        small_lower,
        small_center,
        small_upper,
        pivots,
        eliminating_factor,
    ) = line_factors(viscosity, row_groups, depth_rows)

    def own_entry(table, along_axis):
        return lax.dynamic_index_in_dim(table, place, along_axis, keepdims=False)

    interior_rhs = predictor[:, :inner_rows]
    last_rhs = predictor[:, inner_rows]
    local_part = unrolled_solve(
        own_entry(lower_coef, 1),
        own_entry(center_coef, 1),
        own_entry(upper_coefficient, 1),
        interior_rhs,
        1,
    )
    next_value = passed_along(local_part[:, 0], "wall", -1)
    interface_rhs = (
        last_rhs
        + own_entry(face_last, 0) * local_part[:, inner_rows - 1]
        + own_entry(high_last, 0) * next_value
    )
    lines = interface_rhs.reshape(1, 3 * cells_x, cells_z)
    solved = line_solve(
        lax.all_to_all(lines, "wall", split_axis=1, concat_axis=0, tiled=True),
        small_lower,
        small_center,
        small_upper,
    )
    shifted = jnp.concatenate([jnp.zeros_like(solved[:1]), solved[:-1]], axis=0)
    before_all = lax.all_to_all(shifted, "wall", split_axis=0, concat_axis=1, tiled=True)
    own_all = lax.all_to_all(solved, "wall", split_axis=0, concat_axis=1, tiled=True)
    below_value = before_all.reshape(3, cells_x, cells_z)
    own_value = own_all.reshape(3, cells_x, cells_z)
    lower_neighbour_weight = own_entry(from_below, 1).reshape(1, inner_rows, 1, 1)
    above_weight = own_entry(from_above, 1).reshape(1, inner_rows, 1, 1)
    inside_rows = (
        local_part
        + lower_neighbour_weight * below_value[:, None]
        + above_weight * own_value[:, None]
    )
    velocity_new = jnp.concatenate([inside_rows, own_value[:, None]], axis=1)
    return (predictor, velocity_new)


def solution(mesh):
    return jax.shard_map(
        on_device,
        mesh=mesh,
        in_specs=(P(None, "wall", "stream", "span"), P()),
        out_specs=(P(None, "wall", "stream", "span"), P(None, "wall", "stream", "span")),
        check_vma=False,
    )
```

profile of v0, /device:TPU:1, one launch (start us, length us, event | category | flops | bytes accessed | tf_op | source)
XLA Modules:
  0.0 931.5 jit_solution(16194645011564091098)
XLA Ops:
  0.6 8.9 fusion.705
  9.5 3.5 copy.2149
  13.0 2.1 collective-permute-start
  15.1 3.5 copy.2150
  18.6 1.4 collective-permute-start.1
  20.8 4.5 collective-permute-start.5
  25.3 2.1 collective-permute-start.4
  27.4 4.8 copy.1762
  38.6 1.1 slice_reduce_fusion.270
  39.7 1.1 slice_reduce_fusion.275
  41.3 1.1 slice_reduce_fusion.346
  42.4 1.1 slice_reduce_fusion.351
  50.8 1.1 slice_reduce_fusion.535
  51.8 1.1 slice_reduce_fusion.582
  53.4 1.1 slice_reduce_fusion.611
  54.5 1.1 slice_reduce_fusion.658
  56.1 1.1 slice_reduce_fusion.687
  58.8 1.1 slice_reduce_fusion.763
  64.3 1.1 slice_reduce_fusion.749
  74.3 3.7 multiply_subtract_fusion.655
  78.0 1.8 subtract_divide_fusion.274
  79.8 1.7 subtract_divide_fusion.84
  81.5 3.7 multiply_subtract_fusion.571
  506.3 3.0 copy.1747
  509.3 3.1 copy.1749
  512.4 8.5 pad_maximum_fusion.8
  520.9 3.8 copy.1750
  524.7 5.6 collective-permute-start.2
  530.3 2.1 copy.1752
  532.8 4.6 multiply_bitcast_fusion.2
  537.4 18.6 %collective-permute-done.2 = f32[3,192,3,134]{1,3,2,0:T(8,128)} collective-permute-done((f32[3,192,3,134]{1,3,2,0:T(8,128)}, f32[3,192,3,134]{1,3,2,0:T(8,128)}, u32[]{:S(2)}, u32[]{:S(2)}) %collective-permute-start.2) | collective-permute-done | bytes 926240 | tf_op jit(solution)/shard_map/ppermute | solution.py:19
  556.0 3.0 copy.1751
  559.0 2.6 collective-permute-done.3
  561.5 3.9 copy.1753
  565.4 23.6 %pad_maximum_fusion = (f32[3,192,19,134]{3,2,0,1:T(8,128)}, f32[3,192,19,134]{3,2,0,1:T(8,128)}) fusion(f32[3,192,3,134]{3,2,0,1:T(4,128)S(1)} %copy.1751, f32[3,192,16,3]{3,2,0,1:T(8,128)} %copy.1749, f32[3,192,16,3]{3,2,0,1:T(8,128)} %copy.1747, f32[3,192,3,134]{3,2,0,1:T(4,128)} %copy.1753, f32[3,192,16,128]{3,2,1,0:T(8,128)} %param.6), kind=kLoop, calls=%fused_computation.7 | loop fusion | flops 8798976 | bytes 18524160 | tf_op jit(solution)/shard_map/concatenate | solution.py:20
  589.0 68.1 %fusion.9 = f32[3,192,16,128]{3,2,0,1:T(8,128)} fusion(f32[3,192,16,128]{3,2,0,1:T(8,128)} %copy.1762, f32[3,192,16,3]{3,2,0,1:T(8,128)} %copy.1747, f32[3,192,16,3]{3,2,0,1:T(8,128)} %copy.1749, f32[3,1,16,128]{3,2,0,1:T(8,128)S(1)} %collective-permute-done.5, f32[3,1,16,128]{3,2,0,1:T(8,128)S(1)} %collective-permute-done.4, ...), kind=kLoop, calls=%fused_computation.25 | loop fusion | flops 35389440 | bytes 42737664 | tf_op jit(solution)/shard_map/sub | solution.py:156
  657.1 13.9 %fusion.369 = (f32[3,16,128]{2,1,0:T(8,128)S(1)}, f32[3,16,128]{2,1,0:T(8,128)S(1)}, f32[3,16,128]{2,1,0:T(8,128)S(1)}, f32[3,16,128]{2,1,0:T(8,128)S(1)}, f32[3...) fusion(f32[3,192,16,128]{3,2,0,1:T(8,128)} %fusion.9, ...), kind=kLoop, calls=%fused_computation.764 | loop fusion | flops 356352 | bytes 737436 | tf_op jit(solution)/shard_map/div | solution.py:51
  671.0 84.6 %fusion.117 = (f32[3,16,128]{2,1,0:T(8,128)S(1)}, f32[3,16,128]{2,1,0:T(8,128)S(1)}, f32[3,16,128]{2,1,0:T(8,128)S(1)}, f32[3,16,128]{2,1,0:T(8,128)S(1)}, f32[3...) fusion(f32[3,192,16,128]{3,2,0,1:T(8,128)} %fusion.9, ...), kind=kLoop, calls=%fused_computation.386 | loop fusion | flops 2322432 | bytes 4670448 | tf_op jit(solution)/shard_map/div | solution.py:51
  755.6 43.0 %multiply_subtract_fusion.100 = (f32[3,16,128]{2,1,0:T(8,128)S(1)}, f32[3,16,128]{2,1,0:T(8,128)S(1)}, f32[3,16,128]{2,1,0:T(8,128)S(1)}, f32[3,16,128]{2,1,0:T(...) fusion(f32[]{:T(128)S(6)} %div.3948, ...), kind=kLoop, calls=%fused_computation.921 | loop fusion | flops 2359296 | bytes 3908488 | tf_op jit(solution)/shard_map/sub | solution.py:56
  798.6 31.7 %constant_dynamic-update-slice_fusion.190 = (f32[3,191,16,128]{3,2,0,1:T(8,128)S(1)}, f32[3,16,128]{2,1,0:T(8,128)S(1)}, f32[3,16,128]{2,1,0:T(8,128)S(1)}, f32[...) fusion(f32[3,16,128]{2,1,0:T(8,128)S(1)} %get-tuple-element.193, ...), kind=kLoop, calls=%fused_computation.245 | loop fusion | flops 2138111 | bytes 3736348
  830.3 2.2 collective-permute-start.6
  835.1 2.2 collective-permute-done.6
  837.2 2.6 fusion.25
  839.8 4.5 all-to-all-start
  845.0 4.1 all-to-all-done
  850.3 36.2 %while.36 = (s32[]{:T(128)}, f32[]{:T(128)}, f32[6,128]{1,0:T(8,128)S(1)}, f32[8]{0:T(128)S(1)}, f32[8,6,128]{2,1,0:T(8,128)S(1)}, /*index=5*/f32[8]{0:T(128)S(1...) while((s32[]{:T(128)}, f32[]{:T(128)}, f32[6,128]{1,0:T(8,128)S(1)}, ...), condition=%wide.region_1.2_spmd.clone.clone, body=%wide.region_0.1_spmd.clone.sunk.clone | while | flops 3078 | bytes 16591 | solution.py:72
  887.2 14.5 %while.37 = (s32[]{:T(128)}, f32[6,128]{1,0:T(8,128)S(1)}, f32[8,6,128]{2,1,0:T(8,128)}, f32[8,6,128]{2,1,0:T(8,128)S(1)}, f32[8]{0:T(128)S(1)}) while((s32[]{:T(128)}, f32[6,128]{1,0:T(8,128)S(1)}, f32[8,6,128]{2,1,0:T(8,128)}, f32[8,6,128]{2,1,0:T(8,128)S(1)}, f32[8]{0:T(128)S(1)}) %tuple.2867), condition=%wide.region_3.4_spmd.clone.clone, body=%wide.region_2.3_spmd.clone.sunk.clone | while | flops 2308 | bytes 13931 | solution.py:81
  887.7 1.2 bitcast_dynamic-update-slice_fusion.7
  889.6 1.2 bitcast_dynamic-update-slice_fusion.7
  891.4 1.2 bitcast_dynamic-update-slice_fusion.7
  893.2 1.2 bitcast_dynamic-update-slice_fusion.7
  895.0 1.2 bitcast_dynamic-update-slice_fusion.7
  896.8 1.2 bitcast_dynamic-update-slice_fusion.7
  898.6 1.2 bitcast_dynamic-update-slice_fusion.7
  900.5 1.2 bitcast_dynamic-update-slice_fusion.7
  901.7 4.0 all-to-all-start.2
  905.6 2.0 constant_dynamic-update-slice_fusion.1
  909.0 1.3 all-to-all-done.2
  910.4 4.0 all-to-all-start.1
  914.4 2.0 constant_dynamic-update-slice_fusion
  916.4 5.0 copy.2146
  921.4 4.3 multiply_add_fusion
  925.7 2.6 pad_maximum_fusion.5
  928.4 2.7 copy.2147
  (848 shorter events, 124.4 us)
Async XLA Ops:
  13.0 493.3 %collective-permute-start = (f32[3,192,16,3]{1,2,3,0:T(8,128)S(1)}, f32[3,192,16,3]{1,2,3,0:T(8,128)S(1)}, u32[]{:S(2)}, u32[]{:S(2)}) collective-permute-start(f32[3,192,16,3]{1,2,3,0:T(8,128)S(1)} %copy.2149), channel_id=1, source_target_pairs={{0,8},{8,16},{16,24},{24,0},{1,9},{9,17},{17,25},{25,1},{2,10},{10... | collective-permute-start | bytes 331784 | tf_op jit(solution)/shard_map/ppermute | solution.py:16
  18.6 490.7 %collective-permute-start.1 = (f32[3,192,16,3]{1,2,3,0:T(8,128)S(1)}, f32[3,192,16,3]{1,2,3,0:T(8,128)S(1)}, u32[]{:S(2)}, u32[]{:S(2)}) collective-permute-start(f32[3,192,16,3]{1,2,3,0:T(8,128)S(1)} %copy.2150), channel_id=1, source_target_pairs={{8,0},{16,8},{24,16},{0,24},{9,1},{17,9},{25,17},{1,25},{10,2},{18... | collective-permute-start | bytes 331784 | tf_op jit(solution)/shard_map/ppermute | solution.py:19
  20.8 568.2 %collective-permute-start.5 = (f32[3,1,16,128]{3,2,0,1:T(8,128)S(1)}, f32[3,1,16,128]{3,2,0,1:T(8,128)S(1)}, u32[]{:S(2)}, u32[]{:S(2)}) collective-permute-start(f32[3,1,16,128]{3,2,0,1:T(8,128)S(1)} %get-tuple-element.2529), channel_id=1, source_target_pairs={{0,32},{32,64},{64,96},{96,128},{128,160},{160,192},{192,224},{1,3... | collective-permute-start | bytes 73736 | tf_op jit(solution)/shard_map/ppermute | solution.py:16
  25.3 7.0 copy-start.2
  25.3 563.7 %collective-permute-start.4 = (f32[3,1,16,128]{3,2,0,1:T(8,128)S(1)}, f32[3,1,16,128]{3,2,0,1:T(8,128)S(1)}, u32[]{:S(2)}, u32[]{:S(2)}) collective-permute-start(f32[3,1,16,128]{3,2,0,1:T(8,128)S(1)} %get-tuple-element.2528), channel_id=1, source_target_pairs={{32,0},{64,32},{96,64},{128,96},{160,128},{192,160},{224,192},{33,... | collective-permute-start | bytes 73736 | tf_op jit(solution)/shard_map/ppermute | solution.py:19
  520.9 11.7 %copy-start.3 = (f32[8]{0:T(128)S(1)}, f32[8]{0:T(128)}, u32[]{:S(2)}) copy-start(f32[8]{0:T(128)} %get-tuple-element.3330) | copy-start | bytes 100
  524.7 31.3 %collective-permute-start.2 = (f32[3,192,3,134]{1,3,2,0:T(8,128)}, f32[3,192,3,134]{1,3,2,0:T(8,128)}, u32[]{:S(2)}, u32[]{:S(2)}) collective-permute-start(f32[3,192,3,134]{1,3,2,0:T(8,128)} %copy.1750), channel_id=1, source_target_pairs={{1,0},{2,1},{3,2},{4,3},{5,4},{6,5},{7,6},{0,7},{9,8},{10,9},{11,1... | collective-permute-start | bytes 2778632 | tf_op jit(solution)/shard_map/ppermute | solution.py:19
  532.4 29.1 %collective-permute-start.3 = (f32[3,192,3,134]{1,3,2,0:T(8,128)}, f32[3,192,3,134]{1,3,2,0:T(8,128)}, u32[]{:S(2)}, u32[]{:S(2)}) collective-permute-start(f32[3,192,3,134]{1,3,2,0:T(8,128)} %copy.1752), channel_id=1, source_target_pairs={{0,1},{1,2},{2,3},{3,4},{4,5},{5,6},{6,7},{7,0},{8,9},{9,10},{10,1... | collective-permute-start | bytes 2778632 | tf_op jit(solution)/shard_map/ppermute | solution.py:16
  657.1 98.5 %copy-start = (f32[3,192,16,128]{3,2,0,1:T(8,128)S(1)}, f32[3,192,16,128]{3,2,0,1:T(8,128)}, u32[]{:S(2)}) copy-start(f32[3,192,16,128]{3,2,0,1:T(8,128)} %fusion.9) | copy-start | bytes 14155780
  830.3 7.0 collective-permute-start.6
  833.1 17.2 %copy-start.4 = (f32[8]{0:T(128)S(1)}, f32[8]{0:T(128)}, u32[]{:S(2)}) copy-start(f32[8]{0:T(128)} %custom-call.4) | copy-start | bytes 100
  835.1 4.7 copy-start.1
  839.8 9.2 all-to-all-start
  901.7 8.7 all-to-all-start.2
  910.4 11.0 %all-to-all-start.1 = ((f32[8,6,128]{2,1,0:T(8,128)}), f32[8,6,128]{2,1,0:T(8,128)S(1)}, u32[]{:S(2)}, u32[]{:S(2)}) async-start(f32[8,6,128]{2,1,0:T(8,128)} %concatenate.57), calls=%async_computation.1 | async-start | bytes 65536 | tf_op jit(solution)/shard_map/all_to_all | solution.py:198
where the time goes:
time: 944 us; the launch traced here: 932 us
  between operations  361 us (38%)
  other arithmetic  326 us (35%)
  local copies, waits for them, and re-layouts  170 us (18%)
  starting transfers between devices  30.3 us (3%)
  waiting for transfers between devices  28.8 us (3%)
  loops' own time  15.4 us (2%)
    div x6, other arithmetic, unrolled_solve(): value_now = (rhs_piece - lower_coef[position] * values[-1]) / pivot_value  102 us
    sub x1, other arithmetic, on_device(): predictor = velocity - step_size * advect  68.1 us
    sub x2, other arithmetic, unrolled_solve(): solved.insert(0, values[position] - primes[position] * solved[0])  43 us
    unnamed x98, other arithmetic  34.4 us
    another operation x384, local copies, waits for them, and re-layouts, unrolled_solve(): return jnp.stack(solved, axis=along_axis)  31.4 us
    concatenate x1, other arithmetic, extended(): block = jnp.concatenate([low, block, high], axis=dim)  23.6 us
    unnamed x109, local copies, waits for them, and re-layouts  20.6 us
    slice x22, local copies, waits for them, and re-layouts, unrolled_solve(): pivot_value = center_coef[position] - lower_coef[position] * primes[-1]  19.6 us
  transfers between devices with their start and end apart: 10, of which 5 were waited for; matrix products, arithmetic and copies ran while one was open for 21% of the time, Pallas kernels for 0%

commit v1 on v0

v1 whole, which is shorter than its diff:
```python
import jax
import jax.numpy as jnp
from jax import lax
from jax.experimental import pallas as pl
from jax.experimental.pallas import tpu as pltpu
from jax.sharding import PartitionSpec as P

step_size = 0.5
scale = step_size / 60.0
f32 = jnp.float32
VMEM_SPEC = pl.BlockSpec(memory_space=pltpu.VMEM)
HBM_SPEC = pl.BlockSpec(memory_space=pltpu.HBM)
LIMIT = 12 << 20
hops = (2, 6, 4)


def ring(count, shift):
    return [(i, (i + shift) % count) for i in range(count)]


def call(kernel, outs, in_specs, out_specs, scratch, name, args, cost, aliases=None):
    flops, moved = cost
    return pl.pallas_call(
        kernel,
        out_shape=outs,
        in_specs=in_specs,
        out_specs=out_specs,
        scratch_shapes=scratch,
        name=name,
        input_output_aliases=aliases or {},
        cost_estimate=pl.CostEstimate(flops=flops, bytes_accessed=moved, transcendentals=0),
        compiler_params=pltpu.CompilerParams(vmem_limit_bytes=LIMIT),
    )(*args)


def edge_rows(v_ref, low, high, sems):
    copies = []
    for c in range(3):
        for e in range(3):
            copies.append(pltpu.make_async_copy(v_ref.at[c, :, 13 + e], high.at[c, e], sems.at[c * 3 + e]))
            copies.append(pltpu.make_async_copy(v_ref.at[c, :, e], low.at[c, e], sems.at[9 + c * 3 + e]))
    for copy in copies:
        copy.start()
    for copy in copies:
        copy.wait()


def stage(v_ref, after, padded, z_edges, y_first, y_last, sems):
    copies = []
    for part in range(4):
        for c in range(3):
            rows = pl.ds(part * 768, 768)
            copies.append(
                pltpu.make_async_copy(
                    v_ref.at[c, rows], padded.at[c, pl.ds(16 + part * 768, 768)], sems.at[part * 3 + c]
                )
            )
    for copy in copies:
        copy.start()
    for c in range(3):
        padded[c, 0:16] = jnp.zeros((16, 128), f32)
        padded[c, 3088:3104] = jnp.zeros((16, 128), f32)
    lane = lax.broadcasted_iota(jnp.int32, (8, 128), 1)
    for part in range(4):
        for c in range(3):
            copies[part * 3 + c].wait()

        def body(step, carry):
            for u in range(2):
                t = part * 6 + step * 2 + u
                for c in range(3):
                    pieces = []
                    for i in range(16):
                        f = padded[c, pl.ds(pl.multiple_of(16 + t * 128 + i * 8, 8), 8), :]
                        here = (lane >= 8 * i) & (lane < 8 * i + 8)
                        pieces.append(jnp.where(here, pltpu.roll(f, 8 * i + 3, 1), 0.0))
                    while len(pieces) > 1:
                        pieces = [pieces[k] + pieces[k + 1] for k in range(0, len(pieces), 2)]
                    z_edges[pl.ds(pl.multiple_of(c * 192 + t * 8, 8), 8), :] = pieces[0]
            return carry

        lax.fori_loop(0, 3, body, 0)
    for c in range(3):
        y_first[c] = padded[c, 16:32]
        y_last[c] = padded[c, 3072:3088]


def shifted(value, distance, fill):
    rows, lanes = value.shape
    lane = lax.broadcasted_iota(jnp.int32, value.shape, 1)
    row = lax.broadcasted_iota(jnp.int32, value.shape, 0)
    flat = row * lanes + lane
    whole, part = divmod(abs(distance), lanes)
    if distance > 0:
        out = pltpu.roll(value, whole, 0) if whole else value
        if part:
            out = pltpu.roll(out, part, 1)
            out = jnp.where(lane < part, pltpu.roll(out, 1, 0), out)
        return jnp.where(flat < distance, fill, out)
    out = pltpu.roll(value, rows - whole, 0) if whole else value
    if part:
        out = pltpu.roll(out, lanes - part, 1)
        out = jnp.where(lane >= lanes - part, pltpu.roll(out, rows - 1, 0), out)
    return jnp.where(flat >= rows * lanes + distance, fill, out)


def homogeneous(nu_ref, after, p_ref, q_ref, table, column):
    row = lax.broadcasted_iota(jnp.int32, (16, 128), 0)
    lane = lax.broadcasted_iota(jnp.int32, (16, 128), 1)
    table[...] = jnp.ones((16, 128), f32)
    table[0:12] = nu_ref[...]
    low_face = table[...]
    high_face = shifted(low_face, -1, 1.0)
    high_face = jnp.where((row == 11) & (lane == 127), low_face, high_face)

    def products(face, towards):
        r = jnp.where(row < 12, 1.0 / face, 0.0)
        m = [1.0 + r, r, jnp.where(row < 12, 1.0, 0.0), jnp.ones((16, 128), f32)]
        k = 1
        while k < 1536:
            o = [shifted(v, towards * k, fill) for v, fill in zip(m, (1.0, 0.0, 0.0, 1.0))]
            m = [
                m[0] * o[0] + m[1] * o[2],
                m[0] * o[1] + m[1] * o[3],
                m[2] * o[0] + m[3] * o[2],
                m[2] * o[1] + m[3] * o[3],
            ]
            k *= 2
        return m, r

    before, r_low = products(low_face, 1)
    after_it, r_high = products(high_face, -1)
    p, flux = before[1], before[3]
    last = p + r_high * (flux + p)
    wronskian = jnp.broadcast_to(last[11:12, 127:128], (16, 128))
    place = lax.axis_index("wall")
    first = (place * 3) // 2
    skip = (place % 2) * 64
    sub = lax.broadcasted_iota(jnp.int32, (128, 128), 0)
    across = lax.broadcasted_iota(jnp.int32, (128, 128), 1)
    for values, out in ((p, p_ref), (after_it[1] / wronskian, q_ref)):
        table[...] = values
        for half in range(2):
            line = jnp.broadcast_to(table[pl.ds(first + half, 1), :], (128, 128))
            turned = jnp.sum(jnp.where(sub == across, line, 0.0), axis=1, keepdims=True)
            column[half * 128 : half * 128 + 128] = jnp.broadcast_to(turned, (128, 128))
        out[...] = column[pl.ds(pl.multiple_of(skip, 64), 192), :]


def interior(padded, pred):
    sub = lax.broadcasted_iota(jnp.int32, (8, 128), 0)
    source = lax.broadcasted_iota(jnp.int32, (256, 128), 0) % 128
    target = lax.broadcasted_iota(jnp.int32, (256, 128), 1)
    apart = source - target
    band = jnp.zeros((256, 128), f32)
    for m, weight in ((1, 45.0), (2, -9.0), (3, 1.0)):
        band = jnp.where(apart == m, weight, jnp.where(apart == -m, -weight, band))
    band = band.astype(jnp.bfloat16)

    def body(i, carry):
        base = 16 + i * 128

        def part(comp, offset):
            return padded[comp, pl.ds(base + offset, 8), :]

        def aligned(comp, offset, count):
            return padded[comp, pl.ds(pl.multiple_of(base + offset, 8), count), :]

        speeds = [
            (aligned(0, 8 * h, 8) * scale, aligned(1, 8 * h, 8) * (0.5 * step_size), aligned(2, 8 * h, 8) * scale)
            for h in range(16)
        ]
        for c in range(3):
            f = aligned(c, 0, 128)
            upper = f.astype(jnp.bfloat16)
            lower = (f - upper.astype(f32)).astype(jnp.bfloat16)
            slope_z = jnp.dot(jnp.concatenate([upper, lower], axis=1), band, preferred_element_type=f32)
            for h in range(16):
                slope_x = None
                for m, weight in ((1, 45.0), (2, -9.0), (3, 1.0)):
                    up = part(c, 8 * h + m)
                    down = part(c, 8 * h - m)
                    if h % 2:
                        up = jnp.where(sub < 8 - m, up, 0.0)
                    else:
                        down = jnp.where(sub < m, 0.0, down)
                    term = up - down
                    term = weight * term if weight != 1.0 else term
                    slope_x = term if m == 1 else slope_x + term
                slope_y = aligned(c, 16 + 8 * h, 8) - aligned(c, 8 * h - 16, 8)
                v0, v1, v2 = speeds[h]
                advect = v0 * slope_x + v1 * slope_y + v2 * slope_z[8 * h : 8 * h + 8]
                pred[c, pl.ds(pl.multiple_of(i * 128 + 8 * h, 8), 8), :] = f[8 * h : 8 * h + 8] - advect
        return carry

    lax.fori_loop(0, 24, body, 0)


def patch(pred_in, padded, z_edges, z_next, z_prev, below, above, p_ref, q_ref, pred, a_ref, b_ref, change):
    lane = lax.broadcasted_iota(jnp.int32, (8, 128), 1)
    outer = (lane < 3) | (lane >= 125)
    place = lax.broadcasted_iota(jnp.int32, (192, 128), 1) & 7
    for c in range(3):
        rows = slice(c * 192, c * 192 + 192)
        n = z_next[rows]
        up = pltpu.roll(n, 125, 1)
        up -= jnp.where(place >= 1, 9.0 * pltpu.roll(n, 126, 1), 0.0)
        up += jnp.where(place >= 2, 45.0 * pltpu.roll(n, 127, 1), 0.0)
        n = z_prev[rows]
        down = jnp.where(place <= 4, 9.0 * pltpu.roll(n, 2, 1), 0.0) - pltpu.roll(n, 3, 1)
        down -= jnp.where(place <= 3, 45.0 * pltpu.roll(n, 1, 1), 0.0)
        change[rows] = jnp.where(place < 3, up, down) * (z_edges[384:576] * scale)

    def body(t, carry):
        carry = list(carry)
        for c in range(3):
            packed = change[pl.ds(pl.multiple_of(c * 192 + t * 8, 8), 8), :]
            for i in range(8):
                p = p_ref[pl.ds(t * 8 + i, 1), :]
                q = q_ref[pl.ds(t * 8 + i, 1), :]
                for h in range(2):
                    k = 8 * (2 * i + h) + 3
                    back = jnp.where(outer, pltpu.roll(packed, 128 - k, 1), 0.0)
                    rows = pl.ds(pl.multiple_of(t * 128 + i * 16 + h * 8, 8), 8)
                    now = pred_in[c, rows, :] - back
                    pred[c, rows, :] = now
                    carry[c * 2 + h] = carry[c * 2 + h] + p * now
                    carry[6 + c * 2 + h] = carry[6 + c * 2 + h] + q * now
        return tuple(carry)

    sums = lax.fori_loop(0, 24, body, tuple(jnp.zeros((8, 128), f32) for _ in range(12)))
    for c in range(3):
        low = (0.5 * step_size) * padded[1, 16:32] * below[c]
        high = (0.5 * step_size) * padded[1, 3072:3088] * above[c]
        pred[c, 0:16] += low
        pred[c, 3056:3072] -= high
        for h in range(2):
            at = slice(c * 16 + h * 8, c * 16 + h * 8 + 8)
            half = slice(h * 8, h * 8 + 8)
            a_ref[at] = sums[c * 2 + h] + p_ref[0:1] * low[half] - p_ref[191:192] * high[half]
            b_ref[at] = sums[6 + c * 2 + h] + q_ref[0:1] * low[half] - q_ref[191:192] * high[half]


def faces(got_low, got_high, own_low, own_high, p_ref, q_ref, a_in, b_in, outer, both):
    both[0] = a_in[...]
    both[1] = b_in[...]
    for c in range(3):

        def body(i, carry):
            out = list(carry)
            for u in range(2):
                at = pl.ds(pl.multiple_of(i * 16 + u * 8, 8), 8)
                m3, m2, m1 = (got_low[c, j, at, :] for j in range(3))
                p1, p2, p3 = (got_high[c, j, at, :] for j in range(3))
                slopes = (
                    9.0 * m2 - 45.0 * m1 - m3,
                    9.0 * m1 - m2,
                    -m1,
                    p1,
                    p2 - 9.0 * p1,
                    45.0 * p1 - 9.0 * p2 + p3,
                )
                p = p_ref[at, :]
                q = q_ref[at, :]
                for e in range(6):
                    along = own_low[0, e, at, :] if e < 3 else own_high[0, e - 3, at, :]
                    change = along * slopes[e] * (-scale)
                    outer[c, e, at, :] = change
                    out[e] = out[e] + p * change
                    out[6 + e] = out[6 + e] + q * change
            return tuple(out)

        sums = lax.fori_loop(0, 12, body, tuple(jnp.zeros((8, 128), f32) for _ in range(12)))
        for e in range(6):
            x = e if e < 3 else e + 10
            row = pl.ds(c * 16 + x, 1)
            both[0, row, :] += jnp.sum(sums[e], axis=0, keepdims=True)
            both[1, row, :] += jnp.sum(sums[6 + e], axis=0, keepdims=True)


def local_lines(pred, outer, p_ref, q_ref, out, local, spread, full, sems):
    copies = []
    for c in range(3):

        def clear(i, carry):
            for u in range(8):
                spread[pl.ds(pl.multiple_of(i * 64 + u * 8, 8), 8), :] = jnp.zeros((8, 128), f32)
            return carry

        if c == 0:
            lax.fori_loop(0, 48, clear, 0)

        def widen(i, carry):
            for e in range(6):
                x = e if e < 3 else e + 10
                spread[pl.ds(i * 128 + x, 8, stride=16), :] = outer[c, e, pl.ds(pl.multiple_of(i * 8, 8), 8), :]
            return carry

        lax.fori_loop(0, 24, widen, 0)

        def body(i, carry):
            s, t = carry
            for u in range(8):
                y = i * 8 + u
                p = p_ref[pl.ds(y, 1), :]
                q = q_ref[pl.ds(y, 1), :]
                at = pl.ds(pl.multiple_of(y * 16, 16), 16)
                r = pred[c, at, :] + spread[at, :]
                full[c, at, :] = r
                s = s + p * r
                t = t + q * r
                local[c, at, :] = q * s - p * t
            return s, t

        lax.fori_loop(0, 24, body, tuple(jnp.zeros((16, 128), f32) for _ in range(2)))
        copy = pltpu.make_async_copy(full.at[c], out.at[c], sems.at[c])
        copy.start()
        copies.append(copy)
    for copy in copies:
        copy.wait()


def pairs(both, other, *sent):
    place = lax.axis_index("wall")
    for k, out in zip(hops, sent):
        side = jnp.where(place + k < 8, 0, 1)
        out[...] = both[side] + other[side]


def finish(local, p_ref, q_ref, both, other, got_0, got_1, got_2, out, staged, sems):
    place = lax.axis_index("wall")
    second = place % 2 == 1
    low_all = jnp.where(second, other[0], 0.0)
    high_all = both[1] + jnp.where(second, 0.0, other[1])
    for k, got in zip(hops, (got_0, got_1, got_2)):
        value = got[...]
        low_all += jnp.where(place >= k, value, 0.0)
        high_all += jnp.where(place >= k, 0.0, value)
    low = [low_all[c * 16 : c * 16 + 16] for c in range(3)]
    high = [high_all[c * 16 : c * 16 + 16] for c in range(3)]
    copies = []
    for part in range(6):

        def body(i, carry):
            for u in range(4):
                y = part * 32 + i * 4 + u
                p = p_ref[pl.ds(y, 1), :]
                q = q_ref[pl.ds(y, 1), :]
                at = pl.ds(pl.multiple_of(y * 16, 16), 16)
                for c in range(3):
                    staged[c, at, :] = local[c, at, :] + (q * low[c] + p * high[c])
            return carry

        lax.fori_loop(0, 8, body, 0)
        for c in range(3):
            rows = pl.ds(part * 512, 512)
            copy = pltpu.make_async_copy(staged.at[c, rows], out.at[c, rows], sems.at[part * 3 + c])
            copy.start()
            copies.append(copy)
    for copy in copies:
        copy.wait()


def on_device(velocity, viscosity):
    groups = lax.axis_size("wall")
    spans = lax.axis_size("span")
    streams = lax.axis_size("stream")
    DMA = pltpu.SemaphoreType.DMA
    shape = jax.ShapeDtypeStruct
    block = (3, 3072, 128)

    by_row = pltpu.with_memory_space_constraint(velocity.reshape(3, 192, 16, 1, 128), pltpu.HBM)
    edge = shape((3, 3, 192, 1, 128), f32)
    own_low, own_high = call(
        edge_rows, (edge, edge), [HBM_SPEC], (VMEM_SPEC,) * 2, [DMA((18,))], "edge_rows", (by_row,), (0, 3600000)
    )
    own_low = own_low.reshape(3, 3, 192, 128)
    own_high = own_high.reshape(3, 3, 192, 128)
    got_low = lax.ppermute(own_high, "stream", ring(streams, 1))
    got_high = lax.ppermute(own_low, "stream", ring(streams, -1))

    flat = pltpu.with_memory_space_constraint(velocity.reshape(block), pltpu.HBM)
    packed = shape((576, 128), f32)
    layer = shape((3, 16, 128), f32)
    padded, z_edges, y_first, y_last = call(
        stage,
        (shape((3, 3104, 128), f32), packed, layer, layer),
        [HBM_SPEC, pl.BlockSpec(memory_space=pl.ANY)],
        (VMEM_SPEC,) * 4,
        [DMA((12,))],
        "stage",
        (flat, own_low),
        (9000000, 10000000),
    )
    z_next = lax.ppermute(z_edges, "span", ring(spans, -1))
    z_prev = lax.ppermute(z_edges, "span", ring(spans, 1))
    below = lax.ppermute(y_last, "wall", [(i, i + 1) for i in range(groups - 1)])
    above = lax.ppermute(y_first, "wall", [(i + 1, i) for i in range(groups - 1)])

    own_rows = shape((192, 128), f32)
    p, q = call(
        homogeneous,
        (own_rows, own_rows),
        [VMEM_SPEC, pl.BlockSpec(memory_space=pl.ANY)],
        (VMEM_SPEC,) * 2,
        [pltpu.VMEM((16, 128), f32), pltpu.VMEM((256, 128), f32)],
        "homogeneous",
        (viscosity.reshape(12, 128), z_edges),
        (3000000, 32768),
    )

    sums = shape((48, 128), f32)
    pred = call(
        interior, shape(block, f32), [VMEM_SPEC], VMEM_SPEC, [], "interior", (padded,), (60000000, 10000000)
    )
    pred, a, b = call(
        patch,
        (shape(block, f32), sums, sums),
        [VMEM_SPEC] * 9,
        (VMEM_SPEC,) * 3,
        [pltpu.VMEM((576, 128), f32)],
        "patch",
        (pred, padded, z_edges, z_next, z_prev, below, above, p, q),
        (20000000, 10000000),
        {0: 0},
    )
    outer, both = call(
        faces,
        (shape((3, 6, 192, 128), f32), shape((2, 48, 128), f32)),
        [VMEM_SPEC] * 8,
        (VMEM_SPEC,) * 2,
        [],
        "faces",
        (got_low, got_high, own_low, own_high, p, q, a, b),
        (5000000, 5000000),
    )

    other = lax.ppermute(both, "wall", [(i, i ^ 1) for i in range(groups)])
    sent = call(
        pairs, (sums,) * 3, [VMEM_SPEC] * 2, (VMEM_SPEC,) * 3, [], "pairs", (both, other), (40000, 150000)
    )
    got = [lax.ppermute(value, "wall", ring(groups, k)) for k, value in zip(hops, sent)]

    predictor, local = call(
        local_lines,
        (pltpu.HBM(block, f32), shape(block, f32)),
        [VMEM_SPEC] * 4,
        (HBM_SPEC, VMEM_SPEC),
        [pltpu.VMEM((3072, 128), f32), pltpu.VMEM(block, f32), DMA((3,))],
        "local_lines",
        (pred, outer, p, q),
        (9000000, 14000000),
    )
    velocity_new = call(
        finish,
        pltpu.HBM(block, f32),
        [VMEM_SPEC] * 8,
        HBM_SPEC,
        [pltpu.VMEM(block, f32), DMA((18,))],
        "finish",
        (local, p, q, both, other, *got),
        (5000000, 10000000),
    )
    return predictor.reshape(velocity.shape), velocity_new.reshape(velocity.shape)


def solution(mesh):
    return jax.shard_map(
        on_device,
        mesh=mesh,
        in_specs=(P(None, "wall", "stream", "span"), P()),
        out_specs=(P(None, "wall", "stream", "span"), P(None, "wall", "stream", "span")),
        check_vma=False,
    )
```

time: 944 us -> 49.2 us (0.05); the launches traced: 932 us -> 49.1 us
  between operations: 361 us -> 0.8 us
  other arithmetic: 326 us -> 0 us
  local copies, waits for them, and re-layouts: 170 us -> 0.01 us
  waiting for transfers between devices: 28.8 us -> 2.16 us
  Pallas kernels: 0 us -> 25.2 us
  loops' own time: 15.4 us -> 0 us
    sub x5 -> x0, other arithmetic: 118 us -> none  [the longest x1 68.1 us: on_device(): predictor = velocity - step_size * advect]
    div x6 -> x0, other arithmetic: 102 us -> none  [unrolled_solve(): value_now = (rhs_piece - lower_coef[position] * values[-1]) / pivot_value]
    slice x97 -> x0, local copies, waits for them, and re-layouts: 81.9 us -> none  [the longest x22 19.6 us: unrolled_solve(): pivot_value = center_coef[position] - lower_coef[position] * primes[-1]]
    unnamed x98 -> x0, other arithmetic: 34.4 us -> none
    another operation x387 -> x0, local copies, waits for them, and re-layouts: 32.1 us -> none  [the longest x384 31.4 us: unrolled_solve(): return jnp.stack(solved, axis=along_axis)]
    concatenate x3 -> x0, other arithmetic: 26.9 us -> none  [the longest x1 23.6 us: extended(): block = jnp.concatenate([low, block, high], axis=dim)]
    pallas_call x0 -> x9, Pallas kernels: none -> 25.2 us  [call(): pl.pallas_call(kernel, out_shape=outs, in_specs=in_specs, out_specs=out_s...]
    ppermute x7 -> x10, waiting for transfers between devices: 23.4 us -> 2.16 us  [the longest x1 1.22 us: on_device(): other = lax.ppermute(both, 'wall', [(i, i ^ 1) for i in range(groups)])]
  transfers between devices with their start and end apart: 10 -> 10, of which waited for: 5 -> 2; matrix products, arithmetic and copies ran while one was open for 21% -> 0% of each run, Pallas kernels for 0% -> 41%
where the time goes in v1:
time: 49.2 us; the launch traced here: 49.1 us
  Pallas kernels  25.2 us (51%)
  starting transfers between devices  20.9 us (42%)
  waiting for transfers between devices  2.16 us (4%)
  between operations  0.8 us (2%)
    pallas_call x9, Pallas kernels, call(): pl.pallas_call(kernel, out_shape=outs, in_specs=in_specs, out_specs=out_s...  25.2 us
    ppermute x1, starting transfers between devices, on_device(): got_high = lax.ppermute(own_low, 'stream', ring(streams, -1))  6.48 us
    ppermute x3, starting transfers between devices, on_device(): lax.ppermute(value, 'wall', ring(groups, k))  5.57 us
    ppermute x1, starting transfers between devices, on_device(): lax.ppermute(y_last, 'wall', [(i, i + 1) for i in range(groups - 1)])  4.31 us
    ppermute x1, starting transfers between devices, on_device(): z_next = lax.ppermute(z_edges, 'span', ring(spans, -1))  2.56 us
    ppermute x1, starting transfers between devices, on_device(): lax.ppermute(y_first, 'wall', [(i + 1, i) for i in range(groups - 1)])  1.91 us
    ppermute x1, waiting for transfers between devices, on_device(): other = lax.ppermute(both, 'wall', [(i, i ^ 1) for i in range(groups)])  1.22 us
  transfers between devices with their start and end apart: 10, of which 2 were waited for; matrix products, arithmetic and copies ran while one was open for 0% of the time, Pallas kernels for 41%

profile of v1, /device:TPU:1, one launch (start us, length us, event | category | flops | bytes accessed | tf_op | source)
XLA Modules:
  0.0 49.1 jit_solution(13825231744311392608)
XLA Ops:
  0.6 0.0 copy-start
  0.6 1.9 %edge_rows.1 = (f32[3,3,192,1,128]{4,3,2,1,0:T(1,128)S(1)}, f32[3,3,192,1,128]{4,3,2,1,0:T(1,128)S(1)}) custom-call(f32[3,192,16,1,128]{4,3,2,1,0:T(1,128)} %bitcast.13), custom_call_target="tpu_custom_call" | custom-call | bytes 3600000 | tf_op jit(solution)/shard_map/edge_rows/pallas_call | solution.py:23
  2.5 6.5 %collective-permute-start.5 = (f32[3,3,192,128]{3,2,1,0:T(8,128)S(1)}, f32[3,3,192,128]{3,2,1,0:T(8,128)S(1)}, u32[]{:S(2)}, u32[]{:S(2)}) collective-permute-start(f32[3,3,192,128]{3,2,1,0:T(8,128)S(1)} %bitcast.7), channel_id=1, source_target_pairs={{0,7},{1,0},{2,1},{3,2},{4,3},{5,4},{6,5},{7,6},{8,15},{9,8},{10,9... | collective-permute-start | bytes 2654216 | tf_op jit(solution)/shard_map/ppermute | solution.py:380
  9.0 0.0 collective-permute-start.4
  9.0 3.4 %stage.1 = (f32[3,3104,128]{2,1,0:T(8,128)S(1)}, f32[576,128]{1,0:T(8,128)S(1)}, f32[3,16,128]{2,1,0:T(8,128)S(1)}, f32[3,16,128]{2,1,0:T(8,128)S(1)}) custom-call(f32[3,3072,128]{2,1,0:T(8,128)} %bitcast.14, f32[3,3,192,128]{3,2,1,0:T(8,128)S(1)} %bitcast.8), custom_call_target="tpu_custom_call" | custom-call | flops 9000000 | bytes 10000000 | tf_op jit(solution)/shard_map/stage/pallas_call | solution.py:23
  12.5 2.6 %collective-permute-start = (f32[576,128]{1,0:T(8,128)S(1)}, f32[576,128]{1,0:T(8,128)S(1)}, u32[]{:S(2)}, u32[]{:S(2)}) collective-permute-start(f32[576,128]{1,0:T(8,128)S(1)} %get-tuple-element.22.after.z_edges), channel_id=1, source_target_pairs={{0,24},{8,0},{16,8},{24,16},{1,25},{9,1},{17,9},{25,17},{2,26},{10... | collective-permute-start | bytes 884744 | tf_op jit(solution)/shard_map/ppermute | solution.py:395
  15.0 0.0 collective-permute-start.1
  15.0 4.3 %collective-permute-start.2 = (f32[3,16,128]{2,1,0:T(8,128)S(1)}, f32[3,16,128]{2,1,0:T(8,128)S(1)}, u32[]{:S(2)}, u32[]{:S(2)}) collective-permute-start(f32[3,16,128]{2,1,0:T(8,128)S(1)} %get-tuple-element.23), channel_id=1, source_target_pairs={{0,32},{32,64},{64,96},{96,128},{128,160},{160,192},{192,224},{1,3... | collective-permute-start | bytes 73736 | tf_op jit(solution)/shard_map/ppermute | solution.py:397
  19.3 0.9 %collective-permute-done.2.below = f32[3,16,128]{2,1,0:T(8,128)S(1)} collective-permute-done((f32[3,16,128]{2,1,0:T(8,128)S(1)}, f32[3,16,128]{2,1,0:T(8,128)S(1)}, u32[]{:S(2)}, u32[]{:S(2)}) %collective-permute-start.2) | collective-permute-done | bytes 24608 | tf_op jit(solution)/shard_map/ppermute | solution.py:397
  20.3 1.9 %collective-permute-start.3 = (f32[3,16,128]{2,1,0:T(8,128)S(1)}, f32[3,16,128]{2,1,0:T(8,128)S(1)}, u32[]{:S(2)}, u32[]{:S(2)}) collective-permute-start(f32[3,16,128]{2,1,0:T(8,128)S(1)} %get-tuple-element.24), channel_id=1, source_target_pairs={{32,0},{64,32},{96,64},{128,96},{160,128},{192,160},{224,192},{33,... | collective-permute-start | bytes 73736 | tf_op jit(solution)/shard_map/ppermute | solution.py:398
  22.2 0.0 copy-done
  22.2 0.8 %homogeneous.1 = (f32[192,128]{1,0:T(8,128)S(1)}, f32[192,128]{1,0:T(8,128)S(1)}) custom-call(f32[12,128]{1,0:T(8,128)S(1)} %bitcast.12, f32[576,128]{1,0:T(8,128)S(1)} %get-tuple-element.22.after.z_edges), custom_call_target="tpu_custom_call" | custom-call | flops 3000000 | bytes 32768 | tf_op jit(solution)/shard_map/homogeneous/pallas_call | solution.py:23
  23.0 5.4 %interior.1.pred_in = f32[3,3072,128]{2,1,0:T(8,128)S(1)} custom-call(f32[3,3104,128]{2,1,0:T(8,128)S(1)} %get-tuple-element.21.padded), custom_call_target="tpu_custom_call" | custom-call | flops 60000000 | bytes 10000000 | tf_op jit(solution)/shard_map/interior/pallas_call | solution.py:23
  28.4 0.0 collective-permute-done.3.above
  28.4 0.0 collective-permute-done.z_next
  28.4 0.0 collective-permute-done.1.z_prev
  28.4 6.5 %patch.1 = (f32[3,3072,128]{2,1,0:T(8,128)S(1)}, f32[48,128]{1,0:T(8,128)S(1)}, f32[48,128]{1,0:T(8,128)S(1)}) custom-call(f32[3,3072,128]{2,1,0:T(8,128)S(1)} %interior.1.pred_in, f32[3,3104,128]{2,1,0:T(8,128)S(1)} %get-tuple-element.21.padded, f32[576,128]{1,0:T(8,128)S(1)} %get-tuple-element.22.after.z_edges, ...), custom_call_target="tpu_custom_call", output_to_operand_aliasing={{0}: (0, {})} | custom-call | flops 20000000 | bytes 10000000 | tf_op jit(solution)/shard_map/patch/pallas_call | solution.py:23
  34.9 0.0 collective-permute-done.5.got_high
  34.9 0.0 collective-permute-done.4.got_low
  34.9 0.8 %faces.1 = (f32[3,6,192,128]{3,2,1,0:T(8,128)S(1)}, f32[2,48,128]{2,1,0:T(8,128)S(1)}) custom-call(f32[3,3,192,128]{3,2,1,0:T(8,128)S(1)} %collective-permute-done.4.got_low, f32[3,3,192,128]{3,2,1,0:T(8,128)S(1)} %collective-permute-done.5.got_high, f32[3,3,192,128]{3,2,1,0:T(8,128)S(1)} %bitcast.9, f32[3,3,192,128]{3,2,1,0:T(8,128)S(1)} %bitcast.11, ...), custom_call_target="tpu_custom_call" | custom-call | flops 5000000 | bytes 5000000 | tf_op jit(solution)/shard_map/faces/pallas_call | solution.py:23
  35.7 0.1 collective-permute-start.6
  35.8 1.2 %collective-permute-done.6.other = f32[2,48,128]{2,1,0:T(8,128)S(1)} collective-permute-done((f32[2,48,128]{2,1,0:T(8,128)S(1)}, f32[2,48,128]{2,1,0:T(8,128)S(1)}, u32[]{:S(2)}, u32[]{:S(2)}) %collective-permute-start.6) | collective-permute-done | bytes 49184 | tf_op jit(solution)/shard_map/ppermute | solution.py:438
  37.1 2.5 %collective-permute-start.7 = (f32[48,128]{1,0:T(8,128)S(1)}, f32[48,128]{1,0:T(8,128)S(1)}, u32[]{:S(2)}, u32[]{:S(2)}) collective-permute-start(f32[48,128]{1,0:T(8,128)S(1)} %get-tuple-element.35), channel_id=1, source_target_pairs={{0,64},{32,96},{64,128},{96,160},{128,192},{160,224},{192,0},{224,... | collective-permute-start | bytes 73736 | tf_op jit(solution)/shard_map/ppermute | solution.py:442
  39.6 1.5 %collective-permute-start.8 = (f32[48,128]{1,0:T(8,128)S(1)}, f32[48,128]{1,0:T(8,128)S(1)}, u32[]{:S(2)}, u32[]{:S(2)}) collective-permute-start(f32[48,128]{1,0:T(8,128)S(1)} %get-tuple-element.36), channel_id=1, source_target_pairs={{0,192},{32,224},{64,0},{96,32},{128,64},{160,96},{192,128},{224,1... | collective-permute-start | bytes 73736 | tf_op jit(solution)/shard_map/ppermute | solution.py:442
  41.1 1.6 %collective-permute-start.9 = (f32[48,128]{1,0:T(8,128)S(1)}, f32[48,128]{1,0:T(8,128)S(1)}, u32[]{:S(2)}, u32[]{:S(2)}) collective-permute-start(f32[48,128]{1,0:T(8,128)S(1)} %get-tuple-element.37), channel_id=1, source_target_pairs={{0,128},{32,160},{64,192},{96,224},{128,0},{160,32},{192,64},{224,... | collective-permute-start | bytes 73736 | tf_op jit(solution)/shard_map/ppermute | solution.py:442
  42.6 3.9 %local_lines.1 = (f32[3,3072,128]{2,1,0:T(8,128)}, f32[3,3072,128]{2,1,0:T(8,128)S(1)}) custom-call(f32[3,3072,128]{2,1,0:T(8,128)S(1)} %get-tuple-element.27.pred, f32[3,6,192,128]{3,2,1,0:T(8,128)S(1)} %get-tuple-element.31.outer, f32[192,128]{1,0:T(8,128)S(1)} %get-tuple-element.25.p_ref, f32[192,128]{1,0:T(8,128)S(1)} %get-tuple-element.26.q_ref), custom_call_target="tpu_custom_call" | custom-call | flops 9000000 | bytes 14000000 | tf_op jit(solution)/shard_map/local_lines/pallas_call | solution.py:23
  46.5 0.0 collective-permute-done.7.got_0
  46.5 0.0 collective-permute-done.8.got_1
  46.6 0.0 collective-permute-done.9.got_2
  46.6 2.5 %finish.1 = f32[3,3072,128]{2,1,0:T(8,128)} custom-call(f32[3,3072,128]{2,1,0:T(8,128)S(1)} %get-tuple-element.33.local, f32[192,128]{1,0:T(8,128)S(1)} %get-tuple-element.25.p_ref, f32[192,128]{1,0:T(8,128)S(1)} %get-tuple-element.26.q_ref, f32[2,48,128]{2,1,0:T(8,128)S(1)} %get-tuple-element.34.both, f32[2,48,128]{2,1,0:T(8,128)S(1)} %collective-permute-done.6.other, ...), custom_call_target="tpu_custom_call" | custom-call | flops 5000000 | bytes 10000000 | tf_op jit(solution)/shard_map/finish/pallas_call | solution.py:23
  (1 shorter events, 0.0 us)
Async XLA Ops:
  0.6 21.6 %copy-start = (f32[1536]{0:T(1024)S(1)}, f32[1536]{0:T(1024)}, u32[]{:S(2)}) copy-start(f32[1536]{0:T(1024)} %param.3) | copy-start | bytes 18436
  2.5 32.4 %collective-permute-start.5 = (f32[3,3,192,128]{3,2,1,0:T(8,128)S(1)}, f32[3,3,192,128]{3,2,1,0:T(8,128)S(1)}, u32[]{:S(2)}, u32[]{:S(2)}) collective-permute-start(f32[3,3,192,128]{3,2,1,0:T(8,128)S(1)} %bitcast.7), channel_id=1, source_target_pairs={{0,7},{1,0},{2,1},{3,2},{4,3},{5,4},{6,5},{7,6},{8,15},{9,8},{10,9... | collective-permute-start | bytes 2654216 | tf_op jit(solution)/shard_map/ppermute | solution.py:380
  9.0 25.9 %collective-permute-start.4 = (f32[3,3,192,128]{3,2,1,0:T(8,128)S(1)}, f32[3,3,192,128]{3,2,1,0:T(8,128)S(1)}, u32[]{:S(2)}, u32[]{:S(2)}) collective-permute-start(f32[3,3,192,128]{3,2,1,0:T(8,128)S(1)} %bitcast.10), channel_id=1, source_target_pairs={{0,1},{1,2},{2,3},{3,4},{4,5},{5,6},{6,7},{7,0},{8,9},{9,10},{10,1... | collective-permute-start | bytes 2654216 | tf_op jit(solution)/shard_map/ppermute | solution.py:379
  12.5 15.9 %collective-permute-start = (f32[576,128]{1,0:T(8,128)S(1)}, f32[576,128]{1,0:T(8,128)S(1)}, u32[]{:S(2)}, u32[]{:S(2)}) collective-permute-start(f32[576,128]{1,0:T(8,128)S(1)} %get-tuple-element.22.after.z_edges), channel_id=1, source_target_pairs={{0,24},{8,0},{16,8},{24,16},{1,25},{9,1},{17,9},{25,17},{2,26},{10... | collective-permute-start | bytes 884744 | tf_op jit(solution)/shard_map/ppermute | solution.py:395
  15.0 13.4 %collective-permute-start.1 = (f32[576,128]{1,0:T(8,128)S(1)}, f32[576,128]{1,0:T(8,128)S(1)}, u32[]{:S(2)}, u32[]{:S(2)}) collective-permute-start(f32[576,128]{1,0:T(8,128)S(1)} %get-tuple-element.22.after.z_edges), channel_id=1, source_target_pairs={{0,8},{8,16},{16,24},{24,0},{1,9},{9,17},{17,25},{25,1},{2,10},{10... | collective-permute-start | bytes 884744 | tf_op jit(solution)/shard_map/ppermute | solution.py:396
  15.0 5.2 %collective-permute-start.2 = (f32[3,16,128]{2,1,0:T(8,128)S(1)}, f32[3,16,128]{2,1,0:T(8,128)S(1)}, u32[]{:S(2)}, u32[]{:S(2)}) collective-permute-start(f32[3,16,128]{2,1,0:T(8,128)S(1)} %get-tuple-element.23), channel_id=1, source_target_pairs={{0,32},{32,64},{64,96},{96,128},{128,160},{160,192},{192,224},{1,3... | collective-permute-start | bytes 73736 | tf_op jit(solution)/shard_map/ppermute | solution.py:397
  20.3 8.1 %collective-permute-start.3 = (f32[3,16,128]{2,1,0:T(8,128)S(1)}, f32[3,16,128]{2,1,0:T(8,128)S(1)}, u32[]{:S(2)}, u32[]{:S(2)}) collective-permute-start(f32[3,16,128]{2,1,0:T(8,128)S(1)} %get-tuple-element.24), channel_id=1, source_target_pairs={{32,0},{64,32},{96,64},{128,96},{160,128},{192,160},{224,192},{33,... | collective-permute-start | bytes 73736 | tf_op jit(solution)/shard_map/ppermute | solution.py:398
  35.7 1.3 %collective-permute-start.6 = (f32[2,48,128]{2,1,0:T(8,128)S(1)}, f32[2,48,128]{2,1,0:T(8,128)S(1)}, u32[]{:S(2)}, u32[]{:S(2)}) collective-permute-start(f32[2,48,128]{2,1,0:T(8,128)S(1)} %get-tuple-element.34.both), channel_id=1, source_target_pairs={{0,32},{32,0},{64,96},{96,64},{128,160},{160,128},{192,224},{224,1... | collective-permute-start | bytes 147464 | tf_op jit(solution)/shard_map/ppermute | solution.py:438
  37.1 9.5 %collective-permute-start.7 = (f32[48,128]{1,0:T(8,128)S(1)}, f32[48,128]{1,0:T(8,128)S(1)}, u32[]{:S(2)}, u32[]{:S(2)}) collective-permute-start(f32[48,128]{1,0:T(8,128)S(1)} %get-tuple-element.35), channel_id=1, source_target_pairs={{0,64},{32,96},{64,128},{96,160},{128,192},{160,224},{192,0},{224,... | collective-permute-start | bytes 73736 | tf_op jit(solution)/shard_map/ppermute | solution.py:442
  39.6 7.0 %collective-permute-start.8 = (f32[48,128]{1,0:T(8,128)S(1)}, f32[48,128]{1,0:T(8,128)S(1)}, u32[]{:S(2)}, u32[]{:S(2)}) collective-permute-start(f32[48,128]{1,0:T(8,128)S(1)} %get-tuple-element.36), channel_id=1, source_target_pairs={{0,192},{32,224},{64,0},{96,32},{128,64},{160,96},{192,128},{224,1... | collective-permute-start | bytes 73736 | tf_op jit(solution)/shard_map/ppermute | solution.py:442
  41.1 5.5 %collective-permute-start.9 = (f32[48,128]{1,0:T(8,128)S(1)}, f32[48,128]{1,0:T(8,128)S(1)}, u32[]{:S(2)}, u32[]{:S(2)}) collective-permute-start(f32[48,128]{1,0:T(8,128)S(1)} %get-tuple-element.37), channel_id=1, source_target_pairs={{0,128},{32,160},{64,192},{96,224},{128,0},{160,32},{192,64},{224,... | collective-permute-start | bytes 73736 | tf_op jit(solution)/shard_map/ppermute | solution.py:442

commit v2 on v1

v2 whole, which is shorter than its diff:
```python
import functools

import jax
import jax.numpy as jnp
from jax import lax
from jax.experimental import pallas as pl
from jax.experimental.pallas import tpu as pltpu
from jax.sharding import PartitionSpec as P

step_size = 0.5
scale = step_size / 60.0
f32 = jnp.float32
VMEM_SPEC = pl.BlockSpec(memory_space=pltpu.VMEM)
HBM_SPEC = pl.BlockSpec(memory_space=pltpu.HBM)
LIMIT = 12 << 20
hops = (4, 2, 6)


def ring(count, shift):
    return [(i, (i + shift) % count) for i in range(count)]


def call(kernel, outs, in_specs, out_specs, scratch, name, args, cost, aliases=None):
    flops, moved = cost
    return pl.pallas_call(
        kernel,
        out_shape=outs,
        in_specs=in_specs,
        out_specs=out_specs,
        scratch_shapes=scratch,
        name=name,
        input_output_aliases=aliases or {},
        cost_estimate=pl.CostEstimate(flops=flops, bytes_accessed=moved, transcendentals=0),
        compiler_params=pltpu.CompilerParams(vmem_limit_bytes=LIMIT),
    )(*args)


def edge_rows(v_ref, low, high, sems):
    copies = []
    for c in range(3):
        to = pl.ds(4 + 192 * c, 192)
        copies.append(pltpu.make_async_copy(v_ref.at[c, :, 13:16], high.at[to], sems.at[c]))
        copies.append(pltpu.make_async_copy(v_ref.at[c, :, 0:3], low.at[to], sems.at[3 + c]))
    for copy in copies:
        copy.start()
    for ref in (low, high):
        ref[0:4] = jnp.zeros((4, 3, 1, 128), f32)
        ref[580:584] = jnp.zeros((4, 3, 1, 128), f32)
    for copy in copies:
        copy.wait()


def stage(v_ref, after, z_edges):
    lane = lax.broadcasted_iota(jnp.int32, (8, 128), 1)

    def body(step, carry):
        for u in range(2):
            t = step * 2 + u
            for c in range(3):
                pieces = []
                for i in range(16):
                    f = v_ref[c, pl.ds(pl.multiple_of(t * 128 + i * 8, 8), 8), :]
                    here = (lane >= 8 * i) & (lane < 8 * i + 8)
                    pieces.append(jnp.where(here, pltpu.roll(f, 8 * i + 3, 1), 0.0))
                while len(pieces) > 1:
                    pieces = [pieces[k] + pieces[k + 1] for k in range(0, len(pieces), 2)]
                z_edges[pl.ds(pl.multiple_of(c * 192 + t * 8, 8), 8), :] = pieces[0]
        return carry

    lax.fori_loop(0, 12, body, 0)


def shifted(value, distance, fill):
    rows, lanes = value.shape
    lane = lax.broadcasted_iota(jnp.int32, value.shape, 1)
    row = lax.broadcasted_iota(jnp.int32, value.shape, 0)
    flat = row * lanes + lane
    whole, part = divmod(abs(distance), lanes)
    if distance > 0:
        out = pltpu.roll(value, whole, 0) if whole else value
        if part:
            out = pltpu.roll(out, part, 1)
            out = jnp.where(lane < part, pltpu.roll(out, 1, 0), out)
        return jnp.where(flat < distance, fill, out)
    out = pltpu.roll(value, rows - whole, 0) if whole else value
    if part:
        out = pltpu.roll(out, lanes - part, 1)
        out = jnp.where(lane >= lanes - part, pltpu.roll(out, rows - 1, 0), out)
    return jnp.where(flat >= rows * lanes + distance, fill, out)


def homogeneous(nu_ref, after, p_ref, q_ref, table, column):
    row = lax.broadcasted_iota(jnp.int32, (16, 128), 0)
    lane = lax.broadcasted_iota(jnp.int32, (16, 128), 1)
    table[...] = jnp.ones((16, 128), f32)
    table[0:12] = nu_ref[...]
    low_face = table[...]
    high_face = shifted(low_face, -1, 1.0)
    high_face = jnp.where((row == 11) & (lane == 127), low_face, high_face)

    def products(face, towards):
        r = jnp.where(row < 12, 1.0 / face, 0.0)
        m = [1.0 + r, r, jnp.where(row < 12, 1.0, 0.0), jnp.ones((16, 128), f32)]
        k = 1
        while k < 1536:
            o = [shifted(v, towards * k, fill) for v, fill in zip(m, (1.0, 0.0, 0.0, 1.0))]
            m = [
                m[0] * o[0] + m[1] * o[2],
                m[0] * o[1] + m[1] * o[3],
                m[2] * o[0] + m[3] * o[2],
                m[2] * o[1] + m[3] * o[3],
            ]
            k *= 2
        return m, r

    before, r_low = products(low_face, 1)
    after_it, r_high = products(high_face, -1)
    p, flux = before[1], before[3]
    last = p + r_high * (flux + p)
    wronskian = jnp.broadcast_to(last[11:12, 127:128], (16, 128))
    place = lax.axis_index("wall")
    first = (place * 3) // 2
    skip = (place % 2) * 64
    sub = lax.broadcasted_iota(jnp.int32, (128, 128), 0)
    across = lax.broadcasted_iota(jnp.int32, (128, 128), 1)
    for values, out in ((p, p_ref), (after_it[1] / wronskian, q_ref)):
        table[...] = values
        for half in range(2):
            line = jnp.broadcast_to(table[pl.ds(first + half, 1), :], (128, 128))
            turned = jnp.sum(jnp.where(sub == across, line, 0.0), axis=1, keepdims=True)
            column[half * 128 : half * 128 + 128] = jnp.broadcast_to(turned, (128, 128))
        out[...] = column[pl.ds(pl.multiple_of(skip, 64), 192), :]


def interior(v_ref, after, pred, y_first, y_last):
    sub = lax.broadcasted_iota(jnp.int32, (8, 128), 0)
    source = lax.broadcasted_iota(jnp.int32, (256, 128), 0) % 128
    target = lax.broadcasted_iota(jnp.int32, (256, 128), 1)
    apart = source - target
    band = jnp.zeros((256, 128), f32)
    for m, weight in ((1, 45.0), (2, -9.0), (3, 1.0)):
        band = jnp.where(apart == m, weight, jnp.where(apart == -m, -weight, band))
    band = band.astype(jnp.bfloat16)

    def eight_rows(i, first, last):
        base = i * 128

        def part(comp, offset):
            return v_ref[comp, pl.ds(base + offset, 8), :]

        def aligned(comp, offset, count):
            at = base + offset
            return v_ref[comp, pl.ds(at if isinstance(at, int) else pl.multiple_of(at, 8), count), :]

        speeds = [
            (aligned(0, 8 * h, 8) * scale, aligned(1, 8 * h, 8) * (0.5 * step_size), aligned(2, 8 * h, 8) * scale)
            for h in range(16)
        ]
        for c in range(3):
            f = aligned(c, 0, 128)
            upper = f.astype(jnp.bfloat16)
            lower = (f - upper.astype(f32)).astype(jnp.bfloat16)
            slope_z = jnp.dot(jnp.concatenate([upper, lower], axis=1), band, preferred_element_type=f32)
            for h in range(16):
                here = f[8 * h : 8 * h + 8]
                slope_x = None
                for m, weight in ((1, 45.0), (2, -9.0), (3, 1.0)):
                    up = pltpu.roll(here, 8 - m, 0) if last and h == 15 else part(c, 8 * h + m)
                    down = pltpu.roll(here, m, 0) if first and h == 0 else part(c, 8 * h - m)
                    if h % 2:
                        up = jnp.where(sub < 8 - m, up, 0.0)
                    else:
                        down = jnp.where(sub < m, 0.0, down)
                    term = up - down
                    term = weight * term if weight != 1.0 else term
                    slope_x = term if m == 1 else slope_x + term
                if first and h < 2:
                    slope_y = aligned(c, 16 + 8 * h, 8)
                elif last and h >= 14:
                    slope_y = -aligned(c, 8 * h - 16, 8)
                else:
                    slope_y = aligned(c, 16 + 8 * h, 8) - aligned(c, 8 * h - 16, 8)
                v0, v1, v2 = speeds[h]
                advect = v0 * slope_x + v1 * slope_y + v2 * slope_z[8 * h : 8 * h + 8]
                at = base + 8 * h
                pred[c, pl.ds(at if isinstance(at, int) else pl.multiple_of(at, 8), 8), :] = here - advect

    def body(i, carry):
        eight_rows(i, False, False)
        return carry

    eight_rows(0, True, False)
    lax.fori_loop(1, 23, body, 0)
    eight_rows(23, False, True)
    for c in range(3):
        y_first[c] = v_ref[c, 0:16]
        y_last[c] = v_ref[c, 3056:3072]


def patch(pred_in, z_edges, z_next, z_prev, after, pred, change):
    lane = lax.broadcasted_iota(jnp.int32, (8, 128), 1)
    outer = (lane < 3) | (lane >= 125)
    place = lax.broadcasted_iota(jnp.int32, (192, 128), 1) & 7
    for c in range(3):
        rows = slice(c * 192, c * 192 + 192)
        n = z_next[rows]
        up = pltpu.roll(n, 125, 1)
        up -= jnp.where(place >= 1, 9.0 * pltpu.roll(n, 126, 1), 0.0)
        up += jnp.where(place >= 2, 45.0 * pltpu.roll(n, 127, 1), 0.0)
        n = z_prev[rows]
        down = jnp.where(place <= 4, 9.0 * pltpu.roll(n, 2, 1), 0.0) - pltpu.roll(n, 3, 1)
        down -= jnp.where(place <= 3, 45.0 * pltpu.roll(n, 1, 1), 0.0)
        change[rows] = jnp.where(place < 3, up, down) * (z_edges[384:576] * scale)

    def body(t, carry):
        for c in range(3):
            packed = change[pl.ds(pl.multiple_of(c * 192 + t * 8, 8), 8), :]
            rows = pl.ds(pl.multiple_of(t * 128, 128), 128)
            before = pred_in[c, rows, :]
            now = []
            for i in range(16):
                back = jnp.where(outer, pltpu.roll(packed, 125 - 8 * i, 1), 0.0)
                now.append(before[i * 8 : i * 8 + 8] - back)
            pred[c, rows, :] = jnp.concatenate(now, axis=0)
        return carry

    lax.fori_loop(0, 24, body, 0)


def arrived(got, out):
    pass


def faces(pred_in, v_ref, got_low, got_high, below, above, p_ref, q_ref, pred, both, out, sems):
    sub = lax.broadcasted_iota(jnp.int32, (8, 128), 0)
    low_weights = [jnp.where(sub <= 2 - k, w * scale, 0.0) for k, w in enumerate((-1.0, 9.0, -45.0))]
    high_weights = [jnp.where(sub >= 5 + k, w * scale, 0.0) for k, w in enumerate((1.0, -9.0, 45.0))]

    def eight_rows(i, carry):
        carry = list(carry)
        for c in range(3):
            rows = pl.ds(pl.multiple_of(i * 128, 128), 128)
            before = pred_in[c, rows, :]
            along = v_ref[0, rows, :]
            now = []
            for y in range(8):
                at = 12 + c * 576 + i * 24 + 3 * y
                low = [w * got_low[pl.ds(at + k, 8), :] for k, w in enumerate(low_weights)]
                high = [w * got_high[pl.ds(at - 5 - k, 8), :] for k, w in enumerate(high_weights)]
                p = p_ref[pl.ds(i * 8 + y, 1), :]
                q = q_ref[pl.ds(i * 8 + y, 1), :]
                for h, slope in enumerate((low, high)):
                    here = slice(y * 16 + h * 8, y * 16 + h * 8 + 8)
                    r = before[here] - along[here] * (slope[0] + slope[1] + slope[2])
                    now.append(r)
                    carry[c * 2 + h] = carry[c * 2 + h] + p * r
                    carry[6 + c * 2 + h] = carry[6 + c * 2 + h] + q * r
            pred[c, rows, :] = jnp.concatenate(now, axis=0)
        return tuple(carry)

    sums = lax.fori_loop(0, 12, eight_rows, tuple(jnp.zeros((8, 128), f32) for _ in range(12)))
    lows = [(0.5 * step_size) * v_ref[1, 0:16, :] * below[c] for c in range(3)]
    highs = [(0.5 * step_size) * v_ref[1, 3056:3072, :] * above[c] for c in range(3)]
    copies = []
    for c in range(3):
        pred[c, 0:16] += lows[c]
        copies.append(pltpu.make_async_copy(pred.at[c, 0:1536], out.at[c, 0:1536], sems.at[c]))
        copies[c].start()
    sums = lax.fori_loop(12, 24, eight_rows, sums)
    for c in range(3):
        pred[c, 3056:3072] -= highs[c]
        for h in range(2):
            at = slice(c * 16 + h * 8, c * 16 + h * 8 + 8)
            half = slice(h * 8, h * 8 + 8)
            k = c * 2 + h
            both[0, at] = sums[k] + p_ref[0:1] * lows[c][half] - p_ref[191:192] * highs[c][half]
            both[1, at] = sums[6 + k] + q_ref[0:1] * lows[c][half] - q_ref[191:192] * highs[c][half]
    for copy in copies:
        copy.wait()


def written(start, count, pred, onto, out, token, sems):
    token[...] = jnp.zeros_like(token)
    rows = pl.ds(start, count)
    copies = [pltpu.make_async_copy(pred.at[c, rows], out.at[c, rows], sems.at[c]) for c in range(3)]
    for copy in copies:
        copy.start()
    for copy in copies:
        copy.wait()


def pairs(both, other, after, *sent):
    place = lax.axis_index("wall")
    for k, out in zip(hops, sent):
        side = jnp.where(place + k < 8, 0, 1)
        out[...] = both[side] + other[side]


def finish(pred, p_ref, q_ref, both, other, got_0, got_1, got_2, out, staged, sems):
    place = lax.axis_index("wall")
    second = place % 2 == 1
    low = jnp.where(second, other[0], 0.0)
    high = both[1] + jnp.where(second, 0.0, other[1])
    for k, got in zip(hops, (got_0, got_1, got_2)):
        value = got[...]
        low += jnp.where(place >= k, value, 0.0)
        high += jnp.where(place >= k, 0.0, value)
    carry = tuple(part[c * 16 : c * 16 + 16] for part in (low, high) for c in range(3))
    copies = []
    for part in range(6):

        def body(i, carry):
            carry = list(carry)
            for c in range(3):
                rows = pl.ds(pl.multiple_of(part * 512 + i * 128, 128), 128)
                r = pred[c, rows, :]
                now = []
                for u in range(8):
                    y = part * 32 + i * 8 + u
                    p = p_ref[pl.ds(y, 1), :]
                    q = q_ref[pl.ds(y, 1), :]
                    here = r[u * 16 : u * 16 + 16]
                    carry[c] = carry[c] + p * here
                    carry[3 + c] = carry[3 + c] - q * here
                    now.append(q * carry[c] + p * carry[3 + c])
                staged[c, rows, :] = jnp.concatenate(now, axis=0)
            return tuple(carry)

        carry = lax.fori_loop(0, 4, body, carry)
        for c in range(3):
            rows = pl.ds(part * 512, 512)
            copy = pltpu.make_async_copy(staged.at[c, rows], out.at[c, rows], sems.at[part * 3 + c])
            copy.start()
            copies.append(copy)
    for copy in copies:
        copy.wait()


def on_device(velocity, viscosity):
    groups = lax.axis_size("wall")
    spans = lax.axis_size("span")
    streams = lax.axis_size("stream")
    DMA = pltpu.SemaphoreType.DMA
    shape = jax.ShapeDtypeStruct
    block = (3, 3072, 128)

    ANY = pl.BlockSpec(memory_space=pl.ANY)
    by_row = pltpu.with_memory_space_constraint(velocity.reshape(3, 192, 16, 1, 128), pltpu.HBM)
    edge = shape((584, 3, 1, 128), f32)
    own_low, own_high = call(
        edge_rows, (edge, edge), [HBM_SPEC], (VMEM_SPEC,) * 2, [DMA((6,))], "edge_rows", (by_row,), (0, 3600000)
    )
    got_low = lax.ppermute(own_high.reshape(1752, 128), "stream", ring(streams, 1))
    got_high = lax.ppermute(own_low.reshape(1752, 128), "stream", ring(streams, -1))

    flat = velocity.reshape(block)
    layer = shape((3, 16, 128), f32)
    z_edges = call(
        stage,
        shape((576, 128), f32),
        [VMEM_SPEC, ANY],
        VMEM_SPEC,
        [],
        "stage",
        (flat, own_low),
        (9000000, 10000000),
    )
    z_next = lax.ppermute(z_edges, "span", ring(spans, -1))
    z_prev = lax.ppermute(z_edges, "span", ring(spans, 1))
    sums = shape((48, 128), f32)
    pred, y_first, y_last = call(
        interior,
        (shape(block, f32), layer, layer),
        [VMEM_SPEC, ANY],
        (VMEM_SPEC,) * 3,
        [],
        "interior",
        (flat, z_edges),
        (60000000, 10000000),
    )
    below = lax.ppermute(y_last, "wall", [(i, i + 1) for i in range(groups - 1)])
    above = lax.ppermute(y_first, "wall", [(i + 1, i) for i in range(groups - 1)])

    own_rows = shape((192, 128), f32)
    p, q = call(
        homogeneous,
        (own_rows, own_rows),
        [VMEM_SPEC, ANY],
        (VMEM_SPEC,) * 2,
        [pltpu.VMEM((16, 128), f32), pltpu.VMEM((256, 128), f32)],
        "homogeneous",
        (viscosity.reshape(12, 128), y_first),
        (3000000, 32768),
    )

    pred = call(
        patch,
        shape(block, f32),
        [VMEM_SPEC] * 4 + [ANY],
        VMEM_SPEC,
        [pltpu.VMEM((576, 128), f32)],
        "patch",
        (pred, z_edges, z_next, z_prev, p),
        (20000000, 10000000),
        {0: 0},
    )
    got_low = call(
        arrived, shape(got_low.shape, f32), [VMEM_SPEC], VMEM_SPEC, [], "arrived", (got_low,), (0, 1024), {0: 0}
    )
    pred, both, predictor = call(
        faces,
        (shape(block, f32), shape((2, 48, 128), f32), pltpu.HBM(block, f32)),
        [VMEM_SPEC] * 8,
        (VMEM_SPEC, VMEM_SPEC, HBM_SPEC),
        [DMA((3,))],
        "faces",
        (pred, flat, got_low, got_high, below, above, p, q),
        (20000000, 10000000),
        {0: 0},
    )

    other = lax.ppermute(both, "wall", [(i, i ^ 1) for i in range(groups)])

    def write(onto, start, count):
        return call(
            functools.partial(written, start, count),
            (pltpu.HBM(block, f32), shape((8, 128), f32)),
            [VMEM_SPEC, HBM_SPEC],
            (HBM_SPEC, VMEM_SPEC),
            [DMA((3,))],
            "written",
            (pred, onto),
            (0, count * 3072),
            {1: 0},
        )

    predictor, after = write(predictor, 1536, 768)
    sent = call(
        pairs, (sums,) * 3, [VMEM_SPEC] * 2 + [ANY], (VMEM_SPEC,) * 3, [], "pairs", (both, other, after), (40000, 150000)
    )
    got = [lax.ppermute(value, "wall", ring(groups, k)) for k, value in zip(hops, sent)]
    predictor, after = write(predictor, 2304, 768)
    velocity_new = call(
        finish,
        pltpu.HBM(block, f32),
        [VMEM_SPEC] * 8,
        HBM_SPEC,
        [pltpu.VMEM(block, f32), DMA((18,))],
        "finish",
        (pred, p, q, both, other, *got),
        (9000000, 10000000),
    )
    return predictor.reshape(velocity.shape), velocity_new.reshape(velocity.shape)


def solution(mesh):
    return jax.shard_map(
        on_device,
        mesh=mesh,
        in_specs=(P(None, "wall", "stream", "span"), P()),
        out_specs=(P(None, "wall", "stream", "span"), P(None, "wall", "stream", "span")),
        check_vma=False,
    )
```

time: 49.2 us -> 44.5 us (0.904)
  Pallas kernels: 25.2 us -> 21.3 us
  waiting for transfers between devices: 2.16 us -> 0.2 us
  starting transfers between devices: 20.9 us -> 22 us
    pallas_call x9 -> x11, Pallas kernels: 25.2 us -> 21.3 us  [call(): pl.pallas_call(kernel, out_shape=outs, in_specs=in_specs, out_specs=out_s...]
    ppermute x1, starting transfers between devices: 0.01 us -> 1.29 us  [on_device(): z_prev = lax.ppermute(z_edges, 'span', ring(spans, 1))]
    ppermute x1, starting transfers between devices: 2.56 us -> 1.47 us  [on_device(): z_next = lax.ppermute(z_edges, 'span', ring(spans, -1))]
    ppermute x1, waiting for transfers between devices: 1.22 us -> 0.17 us  [on_device(): other = lax.ppermute(both, 'wall', [(i, i ^ 1) for i in range(groups)])]
    ppermute x1, waiting for transfers between devices: 0.92 us -> 0.01 us  [on_device(): lax.ppermute(y_last, 'wall', [(i, i + 1) for i in range(groups - 1)])]
    ppermute x3, starting transfers between devices: 5.57 us -> 6.06 us  [on_device(): lax.ppermute(value, 'wall', ring(groups, k))]
  transfers between devices with their start and end apart: 10 -> 10, of which waited for: 2 -> 1; matrix products, arithmetic and copies ran while one was open for 0% -> 0% of each run, Pallas kernels for 41% -> 33%
where the time goes in v2:
time: 44.5 us; the launch traced here: 44.4 us
  starting transfers between devices  22 us (49%)
  Pallas kernels  21.3 us (48%)
  between operations  0.82 us (2%)
    pallas_call x11, Pallas kernels, call(): pl.pallas_call(kernel, out_shape=outs, in_specs=in_specs, out_specs=out_s...  21.3 us
    ppermute x3, starting transfers between devices, on_device(): lax.ppermute(value, 'wall', ring(groups, k))  6.06 us
    ppermute x1, starting transfers between devices, on_device(): lax.ppermute(y_last, 'wall', [(i, i + 1) for i in range(groups - 1)])  4.61 us
    ppermute x1, starting transfers between devices, on_device(): lax.ppermute(own_low.reshape(1752, 128), 'stream', ring(streams, -1))  4.03 us
    ppermute x1, starting transfers between devices, on_device(): lax.ppermute(own_high.reshape(1752, 128), 'stream', ring(streams, 1))  2.54 us
    ppermute x1, starting transfers between devices, on_device(): lax.ppermute(y_first, 'wall', [(i + 1, i) for i in range(groups - 1)])  1.92 us
    ppermute x1, starting transfers between devices, on_device(): z_next = lax.ppermute(z_edges, 'span', ring(spans, -1))  1.47 us
    ppermute x1, starting transfers between devices, on_device(): z_prev = lax.ppermute(z_edges, 'span', ring(spans, 1))  1.29 us
  transfers between devices with their start and end apart: 10, of which 1 were waited for; matrix products, arithmetic and copies ran while one was open for 0% of the time, Pallas kernels for 33%

profile of v2, /device:TPU:1, one launch (start us, length us, event | category | flops | bytes accessed | tf_op | source)
XLA Modules:
  0.0 44.4 jit_solution(8647209592481007511)
XLA Ops:
  0.6 0.0 copy-start
  0.6 1.7 %edge_rows.1 = (f32[584,3,1,128]{3,2,1,0:T(1,128)S(1)}, f32[584,3,1,128]{3,2,1,0:T(1,128)S(1)}) custom-call(f32[3,192,16,1,128]{4,3,2,1,0:T(1,128)} %bitcast.7), custom_call_target="tpu_custom_call" | custom-call | bytes 3600000 | tf_op jit(solution)/shard_map/edge_rows/pallas_call | solution.py:25
  2.3 2.5 %collective-permute-start.2 = (f32[1752,128]{1,0:T(8,128)S(1)}, f32[1752,128]{1,0:T(8,128)S(1)}, u32[]{:S(2)}, u32[]{:S(2)}) collective-permute-start(f32[1752,128]{1,0:T(8,128)S(1)} %bitcast.13), channel_id=1, source_target_pairs={{0,1},{1,2},{2,3},{3,4},{4,5},{5,6},{6,7},{7,0},{8,9},{9,10},{10,1... | collective-permute-start | bytes 2691080 | tf_op jit(solution)/shard_map/ppermute | solution.py:353
  4.9 4.0 %collective-permute-start.3 = (f32[1752,128]{1,0:T(8,128)S(1)}, f32[1752,128]{1,0:T(8,128)S(1)}, u32[]{:S(2)}, u32[]{:S(2)}) collective-permute-start(f32[1752,128]{1,0:T(8,128)S(1)} %bitcast.11), channel_id=1, source_target_pairs={{0,7},{1,0},{2,1},{3,2},{4,3},{5,4},{6,5},{7,6},{8,15},{9,8},{10,9... | collective-permute-start | bytes 2691080 | tf_op jit(solution)/shard_map/ppermute | solution.py:354
  8.9 0.0 copy-done
  8.9 0.0 copy-start.1
  8.9 2.1 %stage.1.after.z_edges = f32[576,128]{1,0:T(8,128)S(1)} custom-call(f32[3,3072,128]{2,1,0:T(8,128)S(1)} %bitcast.8, f32[584,3,1,128]{3,2,1,0:T(1,128)S(1)} %get-tuple-element.18.after), custom_call_target="tpu_custom_call" | custom-call | flops 9000000 | bytes 10000000 | tf_op jit(solution)/shard_map/stage/pallas_call | solution.py:25
  11.0 1.3 %collective-permute-start.1 = (f32[576,128]{1,0:T(8,128)S(1)}, f32[576,128]{1,0:T(8,128)S(1)}, u32[]{:S(2)}, u32[]{:S(2)}) collective-permute-start(f32[576,128]{1,0:T(8,128)S(1)} %stage.1.after.z_edges), channel_id=1, source_target_pairs={{0,8},{8,16},{16,24},{24,0},{1,9},{9,17},{17,25},{25,1},{2,10},{10... | collective-permute-start | bytes 884744 | tf_op jit(solution)/shard_map/ppermute | solution.py:369
  12.3 1.5 %collective-permute-start = (f32[576,128]{1,0:T(8,128)S(1)}, f32[576,128]{1,0:T(8,128)S(1)}, u32[]{:S(2)}, u32[]{:S(2)}) collective-permute-start(f32[576,128]{1,0:T(8,128)S(1)} %stage.1.after.z_edges), channel_id=1, source_target_pairs={{0,24},{8,0},{16,8},{24,16},{1,25},{9,1},{17,9},{25,17},{2,26},{10... | collective-permute-start | bytes 884744 | tf_op jit(solution)/shard_map/ppermute | solution.py:368
  13.7 5.6 %interior.1 = (f32[3,3072,128]{2,1,0:T(8,128)S(1)}, f32[3,16,128]{2,1,0:T(8,128)S(1)}, f32[3,16,128]{2,1,0:T(8,128)S(1)}) custom-call(f32[3,3072,128]{2,1,0:T(8,128)S(1)} %bitcast.9, f32[576,128]{1,0:T(8,128)S(1)} %stage.1.after.z_edges), custom_call_target="tpu_custom_call" | custom-call | flops 60000000 | bytes 10000000 | tf_op jit(solution)/shard_map/interior/pallas_call | solution.py:25
  19.4 4.6 %collective-permute-start.4 = (f32[3,16,128]{2,1,0:T(8,128)S(1)}, f32[3,16,128]{2,1,0:T(8,128)S(1)}, u32[]{:S(2)}, u32[]{:S(2)}) collective-permute-start(f32[3,16,128]{2,1,0:T(8,128)S(1)} %get-tuple-element.23), channel_id=1, source_target_pairs={{0,32},{32,64},{64,96},{96,128},{128,160},{160,192},{192,224},{1,3... | collective-permute-start | bytes 73736 | tf_op jit(solution)/shard_map/ppermute | solution.py:381
  24.0 0.0 collective-permute-done.1.z_prev
  24.0 1.9 %collective-permute-start.5 = (f32[3,16,128]{2,1,0:T(8,128)S(1)}, f32[3,16,128]{2,1,0:T(8,128)S(1)}, u32[]{:S(2)}, u32[]{:S(2)}) collective-permute-start(f32[3,16,128]{2,1,0:T(8,128)S(1)} %get-tuple-element.20.after), channel_id=1, source_target_pairs={{32,0},{64,32},{96,64},{128,96},{160,128},{192,160},{224,192},{33,... | collective-permute-start | bytes 73736 | tf_op jit(solution)/shard_map/ppermute | solution.py:382
  25.9 0.0 copy-done.1
  25.9 0.8 %homogeneous.1 = (f32[192,128]{1,0:T(8,128)S(1)}, f32[192,128]{1,0:T(8,128)S(1)}) custom-call(f32[12,128]{1,0:T(8,128)S(1)} %bitcast.12, f32[3,16,128]{2,1,0:T(8,128)S(1)} %get-tuple-element.20.after), custom_call_target="tpu_custom_call" | custom-call | flops 3000000 | bytes 32768 | tf_op jit(solution)/shard_map/homogeneous/pallas_call | solution.py:25
  26.7 0.0 collective-permute-done.z_next
  26.7 3.4 %patch.1.pred_in = f32[3,3072,128]{2,1,0:T(8,128)S(1)} custom-call(f32[3,3072,128]{2,1,0:T(8,128)S(1)} %get-tuple-element.19.pred_in, f32[576,128]{1,0:T(8,128)S(1)} %stage.1.after.z_edges, f32[576,128]{1,0:T(8,128)S(1)} %collective-permute-done.z_next, f32[576,128]{1,0:T(8,128)S(1)} %collective-permute-done.1.z_prev, ...), custom_call_target="tpu_custom_call", output_to_operand_aliasing={{}: (0, {})} | custom-call | flops 20000000 | bytes 10000000 | tf_op jit(solution)/shard_map/patch/pallas_call | solution.py:25
  30.1 0.0 collective-permute-done.2.got
  30.1 0.0 collective-permute-done.4.below
  30.2 0.0 collective-permute-done.5.above
  30.2 0.0 collective-permute-done.3.got_high
  30.2 2.6 %faces.1 = (f32[3,3072,128]{2,1,0:T(8,128)S(1)}, f32[2,48,128]{2,1,0:T(8,128)S(1)}, f32[3,3072,128]{2,1,0:T(8,128)}) custom-call(f32[3,3072,128]{2,1,0:T(8,128)S(1)} %patch.1.pred_in, f32[3,3072,128]{2,1,0:T(8,128)S(1)} %bitcast.10, f32[1752,128]{1,0:T(8,128)S(1)} %arrived.1.got_low, ...), custom_call_target="tpu_custom_call", output_to_operand_aliasing={{0}: (0, {})} | custom-call | flops 20000000 | bytes 10000000 | tf_op jit(solution)/shard_map/faces/pallas_call | solution.py:25
  32.8 0.1 collective-permute-start.6
  32.9 1.0 %written.2 = (f32[3,3072,128]{2,1,0:T(8,128)}, f32[8,128]{1,0:T(8,128)S(1)}) custom-call(f32[3,3072,128]{2,1,0:T(8,128)S(1)} %get-tuple-element.25.pred, f32[3,3072,128]{2,1,0:T(8,128)} %get-tuple-element.26.onto), custom_call_target="tpu_custom_call", output_to_operand_aliasing={{0}: (1, {})} | custom-call | bytes 2359296 | tf_op jit(solution)/shard_map/written/pallas_call | solution.py:25
  33.9 0.2 collective-permute-done.6.other
  34.1 3.4 %collective-permute-start.7 = (f32[48,128]{1,0:T(8,128)S(1)}, f32[48,128]{1,0:T(8,128)S(1)}, u32[]{:S(2)}, u32[]{:S(2)}) collective-permute-start(f32[48,128]{1,0:T(8,128)S(1)} %get-tuple-element.31), channel_id=1, source_target_pairs={{0,128},{32,160},{64,192},{96,224},{128,0},{160,32},{192,64},{224,... | collective-permute-start | bytes 73736 | tf_op jit(solution)/shard_map/ppermute | solution.py:441
  37.5 0.4 collective-permute-start.8
  37.9 2.3 %collective-permute-start.9 = (f32[48,128]{1,0:T(8,128)S(1)}, f32[48,128]{1,0:T(8,128)S(1)}, u32[]{:S(2)}, u32[]{:S(2)}) collective-permute-start(f32[48,128]{1,0:T(8,128)S(1)} %get-tuple-element.33), channel_id=1, source_target_pairs={{0,192},{32,224},{64,0},{96,32},{128,64},{160,96},{192,128},{224,1... | collective-permute-start | bytes 73736 | tf_op jit(solution)/shard_map/ppermute | solution.py:441
  40.2 1.6 %written.3 = (f32[3,3072,128]{2,1,0:T(8,128)}, f32[8,128]{1,0:T(8,128)}) custom-call(f32[3,3072,128]{2,1,0:T(8,128)S(1)} %get-tuple-element.25.pred, f32[3,3072,128]{2,1,0:T(8,128)} %get-tuple-element.27.onto), custom_call_target="tpu_custom_call", output_to_operand_aliasing={{0}: (1, {})} | custom-call | bytes 2359296 | tf_op jit(solution)/shard_map/written/pallas_call | solution.py:25
  41.8 0.0 collective-permute-done.7.got_0
  41.8 0.0 collective-permute-done.8.got_1
  41.8 0.0 collective-permute-done.9.got_2
  41.8 2.5 %finish.1 = f32[3,3072,128]{2,1,0:T(8,128)} custom-call(f32[3,3072,128]{2,1,0:T(8,128)S(1)} %get-tuple-element.25.pred, f32[192,128]{1,0:T(8,128)S(1)} %get-tuple-element.21.after.p_ref, f32[192,128]{1,0:T(8,128)S(1)} %get-tuple-element.24.q_ref, f32[2,48,128]{2,1,0:T(8,128)S(1)} %get-tuple-element.29.both, f32[2,48,128]{2,1,0:T(8,128)S(1)} %collective-permute-done.6.other, ...), custom_call_target="tpu_custom_call" | custom-call | flops 9000000 | bytes 10000000 | tf_op jit(solution)/shard_map/finish/pallas_call | solution.py:25
  (2 shorter events, 0.0 us)
Async XLA Ops:
  0.6 8.3 %copy-start = (f32[3,192,16,128]{3,2,1,0:T(8,128)S(1)}, f32[3,192,16,128]{3,2,1,0:T(8,128)}, u32[]{:S(2)}) copy-start(f32[3,192,16,128]{3,2,1,0:T(8,128)} %param.2) | copy-start | bytes 14155780
  2.3 27.8 %collective-permute-start.2 = (f32[1752,128]{1,0:T(8,128)S(1)}, f32[1752,128]{1,0:T(8,128)S(1)}, u32[]{:S(2)}, u32[]{:S(2)}) collective-permute-start(f32[1752,128]{1,0:T(8,128)S(1)} %bitcast.13), channel_id=1, source_target_pairs={{0,1},{1,2},{2,3},{3,4},{4,5},{5,6},{6,7},{7,0},{8,9},{9,10},{10,1... | collective-permute-start | bytes 2691080 | tf_op jit(solution)/shard_map/ppermute | solution.py:353
  4.9 25.3 %collective-permute-start.3 = (f32[1752,128]{1,0:T(8,128)S(1)}, f32[1752,128]{1,0:T(8,128)S(1)}, u32[]{:S(2)}, u32[]{:S(2)}) collective-permute-start(f32[1752,128]{1,0:T(8,128)S(1)} %bitcast.11), channel_id=1, source_target_pairs={{0,7},{1,0},{2,1},{3,2},{4,3},{5,4},{6,5},{7,6},{8,15},{9,8},{10,9... | collective-permute-start | bytes 2691080 | tf_op jit(solution)/shard_map/ppermute | solution.py:354
  8.9 17.0 %copy-start.1 = (f32[1536]{0:T(1024)S(1)}, f32[1536]{0:T(1024)}, u32[]{:S(2)}) copy-start(f32[1536]{0:T(1024)} %param.3) | copy-start | bytes 18436
  11.0 13.0 %collective-permute-start.1 = (f32[576,128]{1,0:T(8,128)S(1)}, f32[576,128]{1,0:T(8,128)S(1)}, u32[]{:S(2)}, u32[]{:S(2)}) collective-permute-start(f32[576,128]{1,0:T(8,128)S(1)} %stage.1.after.z_edges), channel_id=1, source_target_pairs={{0,8},{8,16},{16,24},{24,0},{1,9},{9,17},{17,25},{25,1},{2,10},{10... | collective-permute-start | bytes 884744 | tf_op jit(solution)/shard_map/ppermute | solution.py:369
  12.3 14.5 %collective-permute-start = (f32[576,128]{1,0:T(8,128)S(1)}, f32[576,128]{1,0:T(8,128)S(1)}, u32[]{:S(2)}, u32[]{:S(2)}) collective-permute-start(f32[576,128]{1,0:T(8,128)S(1)} %stage.1.after.z_edges), channel_id=1, source_target_pairs={{0,24},{8,0},{16,8},{24,16},{1,25},{9,1},{17,9},{25,17},{2,26},{10... | collective-permute-start | bytes 884744 | tf_op jit(solution)/shard_map/ppermute | solution.py:368
  19.4 10.8 %collective-permute-start.4 = (f32[3,16,128]{2,1,0:T(8,128)S(1)}, f32[3,16,128]{2,1,0:T(8,128)S(1)}, u32[]{:S(2)}, u32[]{:S(2)}) collective-permute-start(f32[3,16,128]{2,1,0:T(8,128)S(1)} %get-tuple-element.23), channel_id=1, source_target_pairs={{0,32},{32,64},{64,96},{96,128},{128,160},{160,192},{192,224},{1,3... | collective-permute-start | bytes 73736 | tf_op jit(solution)/shard_map/ppermute | solution.py:381
  24.0 6.2 %collective-permute-start.5 = (f32[3,16,128]{2,1,0:T(8,128)S(1)}, f32[3,16,128]{2,1,0:T(8,128)S(1)}, u32[]{:S(2)}, u32[]{:S(2)}) collective-permute-start(f32[3,16,128]{2,1,0:T(8,128)S(1)} %get-tuple-element.20.after), channel_id=1, source_target_pairs={{32,0},{64,32},{96,64},{128,96},{160,128},{192,160},{224,192},{33,... | collective-permute-start | bytes 73736 | tf_op jit(solution)/shard_map/ppermute | solution.py:382
  32.8 1.3 %collective-permute-start.6 = (f32[2,48,128]{2,1,0:T(8,128)S(1)}, f32[2,48,128]{2,1,0:T(8,128)S(1)}, u32[]{:S(2)}, u32[]{:S(2)}) collective-permute-start(f32[2,48,128]{2,1,0:T(8,128)S(1)} %get-tuple-element.29.both), channel_id=1, source_target_pairs={{0,32},{32,0},{64,96},{96,64},{128,160},{160,128},{192,224},{224,1... | collective-permute-start | bytes 147464 | tf_op jit(solution)/shard_map/ppermute | solution.py:422
  34.1 7.7 %collective-permute-start.7 = (f32[48,128]{1,0:T(8,128)S(1)}, f32[48,128]{1,0:T(8,128)S(1)}, u32[]{:S(2)}, u32[]{:S(2)}) collective-permute-start(f32[48,128]{1,0:T(8,128)S(1)} %get-tuple-element.31), channel_id=1, source_target_pairs={{0,128},{32,160},{64,192},{96,224},{128,0},{160,32},{192,64},{224,... | collective-permute-start | bytes 73736 | tf_op jit(solution)/shard_map/ppermute | solution.py:441
  37.5 4.3 %collective-permute-start.8 = (f32[48,128]{1,0:T(8,128)S(1)}, f32[48,128]{1,0:T(8,128)S(1)}, u32[]{:S(2)}, u32[]{:S(2)}) collective-permute-start(f32[48,128]{1,0:T(8,128)S(1)} %get-tuple-element.32), channel_id=1, source_target_pairs={{0,64},{32,96},{64,128},{96,160},{128,192},{160,224},{192,0},{224,... | collective-permute-start | bytes 73736 | tf_op jit(solution)/shard_map/ppermute | solution.py:441
  37.9 3.9 %collective-permute-start.9 = (f32[48,128]{1,0:T(8,128)S(1)}, f32[48,128]{1,0:T(8,128)S(1)}, u32[]{:S(2)}, u32[]{:S(2)}) collective-permute-start(f32[48,128]{1,0:T(8,128)S(1)} %get-tuple-element.33), channel_id=1, source_target_pairs={{0,192},{32,224},{64,0},{96,32},{128,64},{160,96},{192,128},{224,1... | collective-permute-start | bytes 73736 | tf_op jit(solution)/shard_map/ppermute | solution.py:441

commit v3 on v2

--- a/solution.py
+++ b/solution.py
@@ -13,7 +13,7 @@
 VMEM_SPEC = pl.BlockSpec(memory_space=pltpu.VMEM)
 HBM_SPEC = pl.BlockSpec(memory_space=pltpu.HBM)
 LIMIT = 12 << 20
-hops = (4, 2, 6)
+hops = (2, 4, 6)
 
 
 def ring(count, shift):
@@ -258,15 +258,15 @@
             pred[c, rows, :] = jnp.concatenate(now, axis=0)
         return tuple(carry)
 
-    sums = lax.fori_loop(0, 12, eight_rows, tuple(jnp.zeros((8, 128), f32) for _ in range(12)))
+    sums = lax.fori_loop(0, 8, eight_rows, tuple(jnp.zeros((8, 128), f32) for _ in range(12)))
     lows = [(0.5 * step_size) * v_ref[1, 0:16, :] * below[c] for c in range(3)]
     highs = [(0.5 * step_size) * v_ref[1, 3056:3072, :] * above[c] for c in range(3)]
     copies = []
     for c in range(3):
         pred[c, 0:16] += lows[c]
-        copies.append(pltpu.make_async_copy(pred.at[c, 0:1536], out.at[c, 0:1536], sems.at[c]))
+        copies.append(pltpu.make_async_copy(pred.at[c, 0:1024], out.at[c, 0:1024], sems.at[c]))
         copies[c].start()
-    sums = lax.fori_loop(12, 24, eight_rows, sums)
+    sums = lax.fori_loop(8, 24, eight_rows, sums)
     for c in range(3):
         pred[c, 3056:3072] -= highs[c]
         for h in range(2):
@@ -434,12 +434,12 @@
             {1: 0},
         )
 
-    predictor, after = write(predictor, 1536, 768)
+    predictor, after = write(predictor, 1024, 1024)
     sent = call(
         pairs, (sums,) * 3, [VMEM_SPEC] * 2 + [ANY], (VMEM_SPEC,) * 3, [], "pairs", (both, other, after), (40000, 150000)
     )
     got = [lax.ppermute(value, "wall", ring(groups, k)) for k, value in zip(hops, sent)]
-    predictor, after = write(predictor, 2304, 768)
+    predictor, after = write(predictor, 2048, 1024)
     velocity_new = call(
         finish,
         pltpu.HBM(block, f32),

time: 44.5 us -> 43.9 us (0.987)
  starting transfers between devices: 22 us -> 21.5 us
    ppermute x3, starting transfers between devices: 6.06 us -> 5.58 us  [on_device(): lax.ppermute(value, 'wall', ring(groups, k))]
  transfers between devices with their start and end apart: 10 -> 10, of which waited for: 1 -> 0; matrix products, arithmetic and copies ran while one was open for 0% -> 0% of each run, Pallas kernels for 33% -> 34%
where the time goes in v3:
time: 43.9 us; the launch traced here: 43.8 us
  starting transfers between devices  21.5 us (49%)
  Pallas kernels  21.4 us (49%)
  between operations  0.82 us (2%)
    pallas_call x11, Pallas kernels, call(): pl.pallas_call(kernel, out_shape=outs, in_specs=in_specs, out_specs=out_s...  21.4 us
    ppermute x3, starting transfers between devices, on_device(): lax.ppermute(value, 'wall', ring(groups, k))  5.58 us
    ppermute x1, starting transfers between devices, on_device(): lax.ppermute(y_last, 'wall', [(i, i + 1) for i in range(groups - 1)])  4.61 us
    ppermute x1, starting transfers between devices, on_device(): lax.ppermute(own_low.reshape(1752, 128), 'stream', ring(streams, -1))  4.03 us
    ppermute x1, starting transfers between devices, on_device(): lax.ppermute(own_high.reshape(1752, 128), 'stream', ring(streams, 1))  2.54 us
    ppermute x1, starting transfers between devices, on_device(): lax.ppermute(y_first, 'wall', [(i + 1, i) for i in range(groups - 1)])  1.92 us
    ppermute x1, starting transfers between devices, on_device(): z_next = lax.ppermute(z_edges, 'span', ring(spans, -1))  1.47 us
    ppermute x1, starting transfers between devices, on_device(): z_prev = lax.ppermute(z_edges, 'span', ring(spans, 1))  1.29 us
  transfers between devices with their start and end apart: 10, of which 0 were waited for; matrix products, arithmetic and copies ran while one was open for 0% of the time, Pallas kernels for 34%

profile of v3, /device:TPU:1, one launch (start us, length us, event | category | flops | bytes accessed | tf_op | source)
XLA Modules:
  0.0 43.8 jit_solution(8611564149214165324)
XLA Ops:
  0.6 0.0 copy-start
  0.6 1.7 %edge_rows.1 = (f32[584,3,1,128]{3,2,1,0:T(1,128)S(1)}, f32[584,3,1,128]{3,2,1,0:T(1,128)S(1)}) custom-call(f32[3,192,16,1,128]{4,3,2,1,0:T(1,128)} %bitcast.7), custom_call_target="tpu_custom_call" | custom-call | bytes 3600000 | tf_op jit(solution)/shard_map/edge_rows/pallas_call | solution.py:25
  2.3 2.5 %collective-permute-start.2 = (f32[1752,128]{1,0:T(8,128)S(1)}, f32[1752,128]{1,0:T(8,128)S(1)}, u32[]{:S(2)}, u32[]{:S(2)}) collective-permute-start(f32[1752,128]{1,0:T(8,128)S(1)} %bitcast.13), channel_id=1, source_target_pairs={{0,1},{1,2},{2,3},{3,4},{4,5},{5,6},{6,7},{7,0},{8,9},{9,10},{10,1... | collective-permute-start | bytes 2691080 | tf_op jit(solution)/shard_map/ppermute | solution.py:353
  4.9 4.0 %collective-permute-start.3 = (f32[1752,128]{1,0:T(8,128)S(1)}, f32[1752,128]{1,0:T(8,128)S(1)}, u32[]{:S(2)}, u32[]{:S(2)}) collective-permute-start(f32[1752,128]{1,0:T(8,128)S(1)} %bitcast.11), channel_id=1, source_target_pairs={{0,7},{1,0},{2,1},{3,2},{4,3},{5,4},{6,5},{7,6},{8,15},{9,8},{10,9... | collective-permute-start | bytes 2691080 | tf_op jit(solution)/shard_map/ppermute | solution.py:354
  8.9 0.0 copy-done
  8.9 0.0 copy-start.1
  8.9 2.1 %stage.1.after.z_edges = f32[576,128]{1,0:T(8,128)S(1)} custom-call(f32[3,3072,128]{2,1,0:T(8,128)S(1)} %bitcast.8, f32[584,3,1,128]{3,2,1,0:T(1,128)S(1)} %get-tuple-element.18.after), custom_call_target="tpu_custom_call" | custom-call | flops 9000000 | bytes 10000000 | tf_op jit(solution)/shard_map/stage/pallas_call | solution.py:25
  11.0 1.3 %collective-permute-start.1 = (f32[576,128]{1,0:T(8,128)S(1)}, f32[576,128]{1,0:T(8,128)S(1)}, u32[]{:S(2)}, u32[]{:S(2)}) collective-permute-start(f32[576,128]{1,0:T(8,128)S(1)} %stage.1.after.z_edges), channel_id=1, source_target_pairs={{0,8},{8,16},{16,24},{24,0},{1,9},{9,17},{17,25},{25,1},{2,10},{10... | collective-permute-start | bytes 884744 | tf_op jit(solution)/shard_map/ppermute | solution.py:369
  12.3 1.5 %collective-permute-start = (f32[576,128]{1,0:T(8,128)S(1)}, f32[576,128]{1,0:T(8,128)S(1)}, u32[]{:S(2)}, u32[]{:S(2)}) collective-permute-start(f32[576,128]{1,0:T(8,128)S(1)} %stage.1.after.z_edges), channel_id=1, source_target_pairs={{0,24},{8,0},{16,8},{24,16},{1,25},{9,1},{17,9},{25,17},{2,26},{10... | collective-permute-start | bytes 884744 | tf_op jit(solution)/shard_map/ppermute | solution.py:368
  13.7 5.6 %interior.1 = (f32[3,3072,128]{2,1,0:T(8,128)S(1)}, f32[3,16,128]{2,1,0:T(8,128)S(1)}, f32[3,16,128]{2,1,0:T(8,128)S(1)}) custom-call(f32[3,3072,128]{2,1,0:T(8,128)S(1)} %bitcast.9, f32[576,128]{1,0:T(8,128)S(1)} %stage.1.after.z_edges), custom_call_target="tpu_custom_call" | custom-call | flops 60000000 | bytes 10000000 | tf_op jit(solution)/shard_map/interior/pallas_call | solution.py:25
  19.4 4.6 %collective-permute-start.4 = (f32[3,16,128]{2,1,0:T(8,128)S(1)}, f32[3,16,128]{2,1,0:T(8,128)S(1)}, u32[]{:S(2)}, u32[]{:S(2)}) collective-permute-start(f32[3,16,128]{2,1,0:T(8,128)S(1)} %get-tuple-element.23), channel_id=1, source_target_pairs={{0,32},{32,64},{64,96},{96,128},{128,160},{160,192},{192,224},{1,3... | collective-permute-start | bytes 73736 | tf_op jit(solution)/shard_map/ppermute | solution.py:381
  24.0 0.0 collective-permute-done.1.z_prev
  24.0 1.9 %collective-permute-start.5 = (f32[3,16,128]{2,1,0:T(8,128)S(1)}, f32[3,16,128]{2,1,0:T(8,128)S(1)}, u32[]{:S(2)}, u32[]{:S(2)}) collective-permute-start(f32[3,16,128]{2,1,0:T(8,128)S(1)} %get-tuple-element.20.after), channel_id=1, source_target_pairs={{32,0},{64,32},{96,64},{128,96},{160,128},{192,160},{224,192},{33,... | collective-permute-start | bytes 73736 | tf_op jit(solution)/shard_map/ppermute | solution.py:382
  25.9 0.0 copy-done.1
  25.9 0.8 %homogeneous.1 = (f32[192,128]{1,0:T(8,128)S(1)}, f32[192,128]{1,0:T(8,128)S(1)}) custom-call(f32[12,128]{1,0:T(8,128)S(1)} %bitcast.12, f32[3,16,128]{2,1,0:T(8,128)S(1)} %get-tuple-element.20.after), custom_call_target="tpu_custom_call" | custom-call | flops 3000000 | bytes 32768 | tf_op jit(solution)/shard_map/homogeneous/pallas_call | solution.py:25
  26.7 0.0 collective-permute-done.z_next
  26.7 3.4 %patch.1.pred_in = f32[3,3072,128]{2,1,0:T(8,128)S(1)} custom-call(f32[3,3072,128]{2,1,0:T(8,128)S(1)} %get-tuple-element.19.pred_in, f32[576,128]{1,0:T(8,128)S(1)} %stage.1.after.z_edges, f32[576,128]{1,0:T(8,128)S(1)} %collective-permute-done.z_next, f32[576,128]{1,0:T(8,128)S(1)} %collective-permute-done.1.z_prev, ...), custom_call_target="tpu_custom_call", output_to_operand_aliasing={{}: (0, {})} | custom-call | flops 20000000 | bytes 10000000 | tf_op jit(solution)/shard_map/patch/pallas_call | solution.py:25
  30.1 0.0 collective-permute-done.2.got
  30.1 0.0 collective-permute-done.4.below
  30.2 0.0 collective-permute-done.5.above
  30.2 0.0 collective-permute-done.3.got_high
  30.2 2.3 %faces.1 = (f32[3,3072,128]{2,1,0:T(8,128)S(1)}, f32[2,48,128]{2,1,0:T(8,128)S(1)}, f32[3,3072,128]{2,1,0:T(8,128)}) custom-call(f32[3,3072,128]{2,1,0:T(8,128)S(1)} %patch.1.pred_in, f32[3,3072,128]{2,1,0:T(8,128)S(1)} %bitcast.10, f32[1752,128]{1,0:T(8,128)S(1)} %arrived.1.got_low, ...), custom_call_target="tpu_custom_call", output_to_operand_aliasing={{0}: (0, {})} | custom-call | flops 20000000 | bytes 10000000 | tf_op jit(solution)/shard_map/faces/pallas_call | solution.py:25
  32.5 0.1 collective-permute-start.6
  32.6 1.2 %written.2 = (f32[3,3072,128]{2,1,0:T(8,128)}, f32[8,128]{1,0:T(8,128)S(1)}) custom-call(f32[3,3072,128]{2,1,0:T(8,128)S(1)} %get-tuple-element.25.pred, f32[3,3072,128]{2,1,0:T(8,128)} %get-tuple-element.26.onto), custom_call_target="tpu_custom_call", output_to_operand_aliasing={{0}: (1, {})} | custom-call | bytes 3145728 | tf_op jit(solution)/shard_map/written/pallas_call | solution.py:25
  33.8 0.0 collective-permute-done.6.other
  33.9 1.9 %collective-permute-start.7 = (f32[48,128]{1,0:T(8,128)S(1)}, f32[48,128]{1,0:T(8,128)S(1)}, u32[]{:S(2)}, u32[]{:S(2)}) collective-permute-start(f32[48,128]{1,0:T(8,128)S(1)} %get-tuple-element.31), channel_id=1, source_target_pairs={{0,64},{32,96},{64,128},{96,160},{128,192},{160,224},{192,0},{224,... | collective-permute-start | bytes 73736 | tf_op jit(solution)/shard_map/ppermute | solution.py:441
  35.8 2.6 %collective-permute-start.8 = (f32[48,128]{1,0:T(8,128)S(1)}, f32[48,128]{1,0:T(8,128)S(1)}, u32[]{:S(2)}, u32[]{:S(2)}) collective-permute-start(f32[48,128]{1,0:T(8,128)S(1)} %get-tuple-element.32), channel_id=1, source_target_pairs={{0,128},{32,160},{64,192},{96,224},{128,0},{160,32},{192,64},{224,... | collective-permute-start | bytes 73736 | tf_op jit(solution)/shard_map/ppermute | solution.py:441
  38.4 1.1 %collective-permute-start.9 = (f32[48,128]{1,0:T(8,128)S(1)}, f32[48,128]{1,0:T(8,128)S(1)}, u32[]{:S(2)}, u32[]{:S(2)}) collective-permute-start(f32[48,128]{1,0:T(8,128)S(1)} %get-tuple-element.33), channel_id=1, source_target_pairs={{0,192},{32,224},{64,0},{96,32},{128,64},{160,96},{192,128},{224,1... | collective-permute-start | bytes 73736 | tf_op jit(solution)/shard_map/ppermute | solution.py:441
  39.5 1.8 %written.3 = (f32[3,3072,128]{2,1,0:T(8,128)}, f32[8,128]{1,0:T(8,128)}) custom-call(f32[3,3072,128]{2,1,0:T(8,128)S(1)} %get-tuple-element.25.pred, f32[3,3072,128]{2,1,0:T(8,128)} %get-tuple-element.27.onto), custom_call_target="tpu_custom_call", output_to_operand_aliasing={{0}: (1, {})} | custom-call | bytes 3145728 | tf_op jit(solution)/shard_map/written/pallas_call | solution.py:25
  41.2 0.0 collective-permute-done.7.got_0
  41.2 0.0 collective-permute-done.8.got_1
  41.2 0.0 collective-permute-done.9.got_2
  41.2 2.5 %finish.1 = f32[3,3072,128]{2,1,0:T(8,128)} custom-call(f32[3,3072,128]{2,1,0:T(8,128)S(1)} %get-tuple-element.25.pred, f32[192,128]{1,0:T(8,128)S(1)} %get-tuple-element.21.after.p_ref, f32[192,128]{1,0:T(8,128)S(1)} %get-tuple-element.24.q_ref, f32[2,48,128]{2,1,0:T(8,128)S(1)} %get-tuple-element.29.both, f32[2,48,128]{2,1,0:T(8,128)S(1)} %collective-permute-done.6.other, ...), custom_call_target="tpu_custom_call" | custom-call | flops 9000000 | bytes 10000000 | tf_op jit(solution)/shard_map/finish/pallas_call | solution.py:25
  (2 shorter events, 0.0 us)
Async XLA Ops:
  0.6 8.3 %copy-start = (f32[3,192,16,128]{3,2,1,0:T(8,128)S(1)}, f32[3,192,16,128]{3,2,1,0:T(8,128)}, u32[]{:S(2)}) copy-start(f32[3,192,16,128]{3,2,1,0:T(8,128)} %param.2) | copy-start | bytes 14155780
  2.3 27.8 %collective-permute-start.2 = (f32[1752,128]{1,0:T(8,128)S(1)}, f32[1752,128]{1,0:T(8,128)S(1)}, u32[]{:S(2)}, u32[]{:S(2)}) collective-permute-start(f32[1752,128]{1,0:T(8,128)S(1)} %bitcast.13), channel_id=1, source_target_pairs={{0,1},{1,2},{2,3},{3,4},{4,5},{5,6},{6,7},{7,0},{8,9},{9,10},{10,1... | collective-permute-start | bytes 2691080 | tf_op jit(solution)/shard_map/ppermute | solution.py:353
  4.9 25.3 %collective-permute-start.3 = (f32[1752,128]{1,0:T(8,128)S(1)}, f32[1752,128]{1,0:T(8,128)S(1)}, u32[]{:S(2)}, u32[]{:S(2)}) collective-permute-start(f32[1752,128]{1,0:T(8,128)S(1)} %bitcast.11), channel_id=1, source_target_pairs={{0,7},{1,0},{2,1},{3,2},{4,3},{5,4},{6,5},{7,6},{8,15},{9,8},{10,9... | collective-permute-start | bytes 2691080 | tf_op jit(solution)/shard_map/ppermute | solution.py:354
  8.9 17.0 %copy-start.1 = (f32[1536]{0:T(1024)S(1)}, f32[1536]{0:T(1024)}, u32[]{:S(2)}) copy-start(f32[1536]{0:T(1024)} %param.3) | copy-start | bytes 18436
  11.0 13.0 %collective-permute-start.1 = (f32[576,128]{1,0:T(8,128)S(1)}, f32[576,128]{1,0:T(8,128)S(1)}, u32[]{:S(2)}, u32[]{:S(2)}) collective-permute-start(f32[576,128]{1,0:T(8,128)S(1)} %stage.1.after.z_edges), channel_id=1, source_target_pairs={{0,8},{8,16},{16,24},{24,0},{1,9},{9,17},{17,25},{25,1},{2,10},{10... | collective-permute-start | bytes 884744 | tf_op jit(solution)/shard_map/ppermute | solution.py:369
  12.3 14.5 %collective-permute-start = (f32[576,128]{1,0:T(8,128)S(1)}, f32[576,128]{1,0:T(8,128)S(1)}, u32[]{:S(2)}, u32[]{:S(2)}) collective-permute-start(f32[576,128]{1,0:T(8,128)S(1)} %stage.1.after.z_edges), channel_id=1, source_target_pairs={{0,24},{8,0},{16,8},{24,16},{1,25},{9,1},{17,9},{25,17},{2,26},{10... | collective-permute-start | bytes 884744 | tf_op jit(solution)/shard_map/ppermute | solution.py:368
  19.4 10.8 %collective-permute-start.4 = (f32[3,16,128]{2,1,0:T(8,128)S(1)}, f32[3,16,128]{2,1,0:T(8,128)S(1)}, u32[]{:S(2)}, u32[]{:S(2)}) collective-permute-start(f32[3,16,128]{2,1,0:T(8,128)S(1)} %get-tuple-element.23), channel_id=1, source_target_pairs={{0,32},{32,64},{64,96},{96,128},{128,160},{160,192},{192,224},{1,3... | collective-permute-start | bytes 73736 | tf_op jit(solution)/shard_map/ppermute | solution.py:381
  24.0 6.2 %collective-permute-start.5 = (f32[3,16,128]{2,1,0:T(8,128)S(1)}, f32[3,16,128]{2,1,0:T(8,128)S(1)}, u32[]{:S(2)}, u32[]{:S(2)}) collective-permute-start(f32[3,16,128]{2,1,0:T(8,128)S(1)} %get-tuple-element.20.after), channel_id=1, source_target_pairs={{32,0},{64,32},{96,64},{128,96},{160,128},{192,160},{224,192},{33,... | collective-permute-start | bytes 73736 | tf_op jit(solution)/shard_map/ppermute | solution.py:382
  32.5 1.3 %collective-permute-start.6 = (f32[2,48,128]{2,1,0:T(8,128)S(1)}, f32[2,48,128]{2,1,0:T(8,128)S(1)}, u32[]{:S(2)}, u32[]{:S(2)}) collective-permute-start(f32[2,48,128]{2,1,0:T(8,128)S(1)} %get-tuple-element.29.both), channel_id=1, source_target_pairs={{0,32},{32,0},{64,96},{96,64},{128,160},{160,128},{192,224},{224,1... | collective-permute-start | bytes 147464 | tf_op jit(solution)/shard_map/ppermute | solution.py:422
  33.9 7.3 %collective-permute-start.7 = (f32[48,128]{1,0:T(8,128)S(1)}, f32[48,128]{1,0:T(8,128)S(1)}, u32[]{:S(2)}, u32[]{:S(2)}) collective-permute-start(f32[48,128]{1,0:T(8,128)S(1)} %get-tuple-element.31), channel_id=1, source_target_pairs={{0,64},{32,96},{64,128},{96,160},{128,192},{160,224},{192,0},{224,... | collective-permute-start | bytes 73736 | tf_op jit(solution)/shard_map/ppermute | solution.py:441
  35.8 5.5 %collective-permute-start.8 = (f32[48,128]{1,0:T(8,128)S(1)}, f32[48,128]{1,0:T(8,128)S(1)}, u32[]{:S(2)}, u32[]{:S(2)}) collective-permute-start(f32[48,128]{1,0:T(8,128)S(1)} %get-tuple-element.32), channel_id=1, source_target_pairs={{0,128},{32,160},{64,192},{96,224},{128,0},{160,32},{192,64},{224,... | collective-permute-start | bytes 73736 | tf_op jit(solution)/shard_map/ppermute | solution.py:441
  38.4 2.9 %collective-permute-start.9 = (f32[48,128]{1,0:T(8,128)S(1)}, f32[48,128]{1,0:T(8,128)S(1)}, u32[]{:S(2)}, u32[]{:S(2)}) collective-permute-start(f32[48,128]{1,0:T(8,128)S(1)} %get-tuple-element.33), channel_id=1, source_target_pairs={{0,192},{32,224},{64,0},{96,32},{128,64},{160,96},{192,128},{224,1... | collective-permute-start | bytes 73736 | tf_op jit(solution)/shard_map/ppermute | solution.py:441

commit v4 on v3

--- a/solution.py
+++ b/solution.py
@@ -54,8 +54,8 @@
     lane = lax.broadcasted_iota(jnp.int32, (8, 128), 1)
 
     def body(step, carry):
-        for u in range(2):
-            t = step * 2 + u
+        for u in range(4):
+            t = step * 4 + u
             for c in range(3):
                 pieces = []
                 for i in range(16):
@@ -67,7 +67,7 @@
                 z_edges[pl.ds(pl.multiple_of(c * 192 + t * 8, 8), 8), :] = pieces[0]
         return carry
 
-    lax.fori_loop(0, 12, body, 0)
+    lax.fori_loop(0, 6, body, 0)
 
 
 def shifted(value, distance, fill):
@@ -212,19 +212,20 @@
         down -= jnp.where(place <= 3, 45.0 * pltpu.roll(n, 1, 1), 0.0)
         change[rows] = jnp.where(place < 3, up, down) * (z_edges[384:576] * scale)
 
-    def body(t, carry):
-        for c in range(3):
-            packed = change[pl.ds(pl.multiple_of(c * 192 + t * 8, 8), 8), :]
-            rows = pl.ds(pl.multiple_of(t * 128, 128), 128)
-            before = pred_in[c, rows, :]
-            now = []
-            for i in range(16):
-                back = jnp.where(outer, pltpu.roll(packed, 125 - 8 * i, 1), 0.0)
-                now.append(before[i * 8 : i * 8 + 8] - back)
-            pred[c, rows, :] = jnp.concatenate(now, axis=0)
+    def body(i, carry):
+        for t in (2 * i, 2 * i + 1):
+            for c in range(3):
+                packed = change[pl.ds(pl.multiple_of(c * 192 + t * 8, 8), 8), :]
+                rows = pl.ds(pl.multiple_of(t * 128, 128), 128)
+                before = pred_in[c, rows, :]
+                now = []
+                for k in range(16):
+                    back = jnp.where(outer, pltpu.roll(packed, 125 - 8 * k, 1), 0.0)
+                    now.append(before[k * 8 : k * 8 + 8] - back)
+                pred[c, rows, :] = jnp.concatenate(now, axis=0)
         return carry
 
-    lax.fori_loop(0, 24, body, 0)
+    lax.fori_loop(0, 12, body, 0)
 
 
 def arrived(got, out):

time: 43.9 us -> 42.9 us (0.977)
  Pallas kernels: 21.4 us -> 20.1 us
    pallas_call x11, Pallas kernels: 21.4 us -> 20.1 us  [call(): pl.pallas_call(kernel, out_shape=outs, in_specs=in_specs, out_specs=out_s...]
    ppermute x1, starting transfers between devices: 0.09 us -> 0.76 us  [on_device(): other = lax.ppermute(both, 'wall', [(i, i ^ 1) for i in range(groups)])]
    ppermute x3, starting transfers between devices: 5.58 us -> 5.06 us  [on_device(): lax.ppermute(value, 'wall', ring(groups, k))]
  transfers between devices with their start and end apart: 10 -> 10, of which waited for: 0 -> 1; matrix products, arithmetic and copies ran while one was open for 0% -> 0% of each run, Pallas kernels for 34% -> 32%
where the time goes in v4:
time: 42.9 us; the launch traced here: 42.7 us
  starting transfers between devices  21.7 us (51%)
  Pallas kernels  20.1 us (47%)
  between operations  0.81 us (2%)
    pallas_call x11, Pallas kernels, call(): pl.pallas_call(kernel, out_shape=outs, in_specs=in_specs, out_specs=out_s...  20.1 us
    ppermute x3, starting transfers between devices, on_device(): lax.ppermute(value, 'wall', ring(groups, k))  5.06 us
    ppermute x1, starting transfers between devices, on_device(): lax.ppermute(y_last, 'wall', [(i, i + 1) for i in range(groups - 1)])  4.61 us
    ppermute x1, starting transfers between devices, on_device(): lax.ppermute(own_low.reshape(1752, 128), 'stream', ring(streams, -1))  4.03 us
    ppermute x1, starting transfers between devices, on_device(): lax.ppermute(own_high.reshape(1752, 128), 'stream', ring(streams, 1))  2.54 us
    ppermute x1, starting transfers between devices, on_device(): lax.ppermute(y_first, 'wall', [(i + 1, i) for i in range(groups - 1)])  1.92 us
    ppermute x1, starting transfers between devices, on_device(): z_next = lax.ppermute(z_edges, 'span', ring(spans, -1))  1.47 us
    ppermute x1, starting transfers between devices, on_device(): z_prev = lax.ppermute(z_edges, 'span', ring(spans, 1))  1.29 us
  transfers between devices with their start and end apart: 10, of which 1 were waited for; matrix products, arithmetic and copies ran while one was open for 0% of the time, Pallas kernels for 32%

profile of v4, /device:TPU:1, one launch (start us, length us, event | category | flops | bytes accessed | tf_op | source)
XLA Modules:
  0.0 42.7 jit_solution(6551972528802081634)
XLA Ops:
  0.6 0.0 copy-start
  0.6 1.7 %edge_rows.1 = (f32[584,3,1,128]{3,2,1,0:T(1,128)S(1)}, f32[584,3,1,128]{3,2,1,0:T(1,128)S(1)}) custom-call(f32[3,192,16,1,128]{4,3,2,1,0:T(1,128)} %bitcast.7), custom_call_target="tpu_custom_call" | custom-call | bytes 3600000 | tf_op jit(solution)/shard_map/edge_rows/pallas_call | solution.py:25
  2.3 2.5 %collective-permute-start.2 = (f32[1752,128]{1,0:T(8,128)S(1)}, f32[1752,128]{1,0:T(8,128)S(1)}, u32[]{:S(2)}, u32[]{:S(2)}) collective-permute-start(f32[1752,128]{1,0:T(8,128)S(1)} %bitcast.13), channel_id=1, source_target_pairs={{0,1},{1,2},{2,3},{3,4},{4,5},{5,6},{6,7},{7,0},{8,9},{9,10},{10,1... | collective-permute-start | bytes 2691080 | tf_op jit(solution)/shard_map/ppermute | solution.py:354
  4.9 4.0 %collective-permute-start.3 = (f32[1752,128]{1,0:T(8,128)S(1)}, f32[1752,128]{1,0:T(8,128)S(1)}, u32[]{:S(2)}, u32[]{:S(2)}) collective-permute-start(f32[1752,128]{1,0:T(8,128)S(1)} %bitcast.11), channel_id=1, source_target_pairs={{0,7},{1,0},{2,1},{3,2},{4,3},{5,4},{6,5},{7,6},{8,15},{9,8},{10,9... | collective-permute-start | bytes 2691080 | tf_op jit(solution)/shard_map/ppermute | solution.py:355
  8.9 0.0 copy-done
  8.9 0.0 copy-start.1
  8.9 1.6 %stage.1.after.z_edges = f32[576,128]{1,0:T(8,128)S(1)} custom-call(f32[3,3072,128]{2,1,0:T(8,128)S(1)} %bitcast.8, f32[584,3,1,128]{3,2,1,0:T(1,128)S(1)} %get-tuple-element.18.after), custom_call_target="tpu_custom_call" | custom-call | flops 9000000 | bytes 10000000 | tf_op jit(solution)/shard_map/stage/pallas_call | solution.py:25
  10.5 1.3 %collective-permute-start.1 = (f32[576,128]{1,0:T(8,128)S(1)}, f32[576,128]{1,0:T(8,128)S(1)}, u32[]{:S(2)}, u32[]{:S(2)}) collective-permute-start(f32[576,128]{1,0:T(8,128)S(1)} %stage.1.after.z_edges), channel_id=1, source_target_pairs={{0,8},{8,16},{16,24},{24,0},{1,9},{9,17},{17,25},{25,1},{2,10},{10... | collective-permute-start | bytes 884744 | tf_op jit(solution)/shard_map/ppermute | solution.py:370
  11.8 1.5 %collective-permute-start = (f32[576,128]{1,0:T(8,128)S(1)}, f32[576,128]{1,0:T(8,128)S(1)}, u32[]{:S(2)}, u32[]{:S(2)}) collective-permute-start(f32[576,128]{1,0:T(8,128)S(1)} %stage.1.after.z_edges), channel_id=1, source_target_pairs={{0,24},{8,0},{16,8},{24,16},{1,25},{9,1},{17,9},{25,17},{2,26},{10... | collective-permute-start | bytes 884744 | tf_op jit(solution)/shard_map/ppermute | solution.py:369
  13.3 5.6 %interior.1 = (f32[3,3072,128]{2,1,0:T(8,128)S(1)}, f32[3,16,128]{2,1,0:T(8,128)S(1)}, f32[3,16,128]{2,1,0:T(8,128)S(1)}) custom-call(f32[3,3072,128]{2,1,0:T(8,128)S(1)} %bitcast.9, f32[576,128]{1,0:T(8,128)S(1)} %stage.1.after.z_edges), custom_call_target="tpu_custom_call" | custom-call | flops 60000000 | bytes 10000000 | tf_op jit(solution)/shard_map/interior/pallas_call | solution.py:25
  18.9 4.6 %collective-permute-start.4 = (f32[3,16,128]{2,1,0:T(8,128)S(1)}, f32[3,16,128]{2,1,0:T(8,128)S(1)}, u32[]{:S(2)}, u32[]{:S(2)}) collective-permute-start(f32[3,16,128]{2,1,0:T(8,128)S(1)} %get-tuple-element.23), channel_id=1, source_target_pairs={{0,32},{32,64},{64,96},{96,128},{128,160},{160,192},{192,224},{1,3... | collective-permute-start | bytes 73736 | tf_op jit(solution)/shard_map/ppermute | solution.py:382
  23.6 0.0 collective-permute-done.1.z_prev
  23.6 1.9 %collective-permute-start.5 = (f32[3,16,128]{2,1,0:T(8,128)S(1)}, f32[3,16,128]{2,1,0:T(8,128)S(1)}, u32[]{:S(2)}, u32[]{:S(2)}) collective-permute-start(f32[3,16,128]{2,1,0:T(8,128)S(1)} %get-tuple-element.20.after), channel_id=1, source_target_pairs={{32,0},{64,32},{96,64},{128,96},{160,128},{192,160},{224,192},{33,... | collective-permute-start | bytes 73736 | tf_op jit(solution)/shard_map/ppermute | solution.py:383
  25.5 0.0 copy-done.1
  25.5 0.8 %homogeneous.1 = (f32[192,128]{1,0:T(8,128)S(1)}, f32[192,128]{1,0:T(8,128)S(1)}) custom-call(f32[12,128]{1,0:T(8,128)S(1)} %bitcast.12, f32[3,16,128]{2,1,0:T(8,128)S(1)} %get-tuple-element.20.after), custom_call_target="tpu_custom_call" | custom-call | flops 3000000 | bytes 32768 | tf_op jit(solution)/shard_map/homogeneous/pallas_call | solution.py:25
  26.3 0.0 collective-permute-done.z_next
  26.3 2.6 %patch.1.pred_in = f32[3,3072,128]{2,1,0:T(8,128)S(1)} custom-call(f32[3,3072,128]{2,1,0:T(8,128)S(1)} %get-tuple-element.19.pred_in, f32[576,128]{1,0:T(8,128)S(1)} %stage.1.after.z_edges, f32[576,128]{1,0:T(8,128)S(1)} %collective-permute-done.z_next, f32[576,128]{1,0:T(8,128)S(1)} %collective-permute-done.1.z_prev, ...), custom_call_target="tpu_custom_call", output_to_operand_aliasing={{}: (0, {})} | custom-call | flops 20000000 | bytes 10000000 | tf_op jit(solution)/shard_map/patch/pallas_call | solution.py:25
  28.9 0.0 collective-permute-done.2.got
  28.9 0.0 collective-permute-done.4.below
  28.9 0.1 collective-permute-done.5.above
  29.0 0.0 collective-permute-done.3.got_high
  29.0 2.3 %faces.1 = (f32[3,3072,128]{2,1,0:T(8,128)S(1)}, f32[2,48,128]{2,1,0:T(8,128)S(1)}, f32[3,3072,128]{2,1,0:T(8,128)}) custom-call(f32[3,3072,128]{2,1,0:T(8,128)S(1)} %patch.1.pred_in, f32[3,3072,128]{2,1,0:T(8,128)S(1)} %bitcast.10, f32[1752,128]{1,0:T(8,128)S(1)} %arrived.1.got_low, ...), custom_call_target="tpu_custom_call", output_to_operand_aliasing={{0}: (0, {})} | custom-call | flops 20000000 | bytes 10000000 | tf_op jit(solution)/shard_map/faces/pallas_call | solution.py:25
  31.4 0.8 %collective-permute-start.6 = (f32[2,48,128]{2,1,0:T(8,128)S(1)}, f32[2,48,128]{2,1,0:T(8,128)S(1)}, u32[]{:S(2)}, u32[]{:S(2)}) collective-permute-start(f32[2,48,128]{2,1,0:T(8,128)S(1)} %get-tuple-element.29.both), channel_id=1, source_target_pairs={{0,32},{32,0},{64,96},{96,64},{128,160},{160,128},{192,224},{224,1... | collective-permute-start | bytes 147464 | tf_op jit(solution)/shard_map/ppermute | solution.py:423
  32.1 1.2 %written.2 = (f32[3,3072,128]{2,1,0:T(8,128)}, f32[8,128]{1,0:T(8,128)S(1)}) custom-call(f32[3,3072,128]{2,1,0:T(8,128)S(1)} %get-tuple-element.25.pred, f32[3,3072,128]{2,1,0:T(8,128)} %get-tuple-element.26.onto), custom_call_target="tpu_custom_call", output_to_operand_aliasing={{0}: (1, {})} | custom-call | bytes 3145728 | tf_op jit(solution)/shard_map/written/pallas_call | solution.py:25
  33.3 0.0 collective-permute-done.6.other
  33.3 1.4 %collective-permute-start.7 = (f32[48,128]{1,0:T(8,128)S(1)}, f32[48,128]{1,0:T(8,128)S(1)}, u32[]{:S(2)}, u32[]{:S(2)}) collective-permute-start(f32[48,128]{1,0:T(8,128)S(1)} %get-tuple-element.31), channel_id=1, source_target_pairs={{0,64},{32,96},{64,128},{96,160},{128,192},{160,224},{192,0},{224,... | collective-permute-start | bytes 73736 | tf_op jit(solution)/shard_map/ppermute | solution.py:442
  34.7 2.6 %collective-permute-start.8 = (f32[48,128]{1,0:T(8,128)S(1)}, f32[48,128]{1,0:T(8,128)S(1)}, u32[]{:S(2)}, u32[]{:S(2)}) collective-permute-start(f32[48,128]{1,0:T(8,128)S(1)} %get-tuple-element.32), channel_id=1, source_target_pairs={{0,128},{32,160},{64,192},{96,224},{128,0},{160,32},{192,64},{224,... | collective-permute-start | bytes 73736 | tf_op jit(solution)/shard_map/ppermute | solution.py:442
  37.3 1.1 %collective-permute-start.9 = (f32[48,128]{1,0:T(8,128)S(1)}, f32[48,128]{1,0:T(8,128)S(1)}, u32[]{:S(2)}, u32[]{:S(2)}) collective-permute-start(f32[48,128]{1,0:T(8,128)S(1)} %get-tuple-element.33), channel_id=1, source_target_pairs={{0,192},{32,224},{64,0},{96,32},{128,64},{160,96},{192,128},{224,1... | collective-permute-start | bytes 73736 | tf_op jit(solution)/shard_map/ppermute | solution.py:442
  38.4 1.8 %written.3 = (f32[3,3072,128]{2,1,0:T(8,128)}, f32[8,128]{1,0:T(8,128)}) custom-call(f32[3,3072,128]{2,1,0:T(8,128)S(1)} %get-tuple-element.25.pred, f32[3,3072,128]{2,1,0:T(8,128)} %get-tuple-element.27.onto), custom_call_target="tpu_custom_call", output_to_operand_aliasing={{0}: (1, {})} | custom-call | bytes 3145728 | tf_op jit(solution)/shard_map/written/pallas_call | solution.py:25
  40.2 0.0 collective-permute-done.7.got_0
  40.2 0.0 collective-permute-done.8.got_1
  40.2 0.0 collective-permute-done.9.got_2
  40.2 2.5 %finish.1 = f32[3,3072,128]{2,1,0:T(8,128)} custom-call(f32[3,3072,128]{2,1,0:T(8,128)S(1)} %get-tuple-element.25.pred, f32[192,128]{1,0:T(8,128)S(1)} %get-tuple-element.21.after.p_ref, f32[192,128]{1,0:T(8,128)S(1)} %get-tuple-element.24.q_ref, f32[2,48,128]{2,1,0:T(8,128)S(1)} %get-tuple-element.29.both, f32[2,48,128]{2,1,0:T(8,128)S(1)} %collective-permute-done.6.other, ...), custom_call_target="tpu_custom_call" | custom-call | flops 9000000 | bytes 10000000 | tf_op jit(solution)/shard_map/finish/pallas_call | solution.py:25
  (2 shorter events, 0.0 us)
Async XLA Ops:
  0.6 8.3 %copy-start = (f32[3,192,16,128]{3,2,1,0:T(8,128)S(1)}, f32[3,192,16,128]{3,2,1,0:T(8,128)}, u32[]{:S(2)}) copy-start(f32[3,192,16,128]{3,2,1,0:T(8,128)} %param.2) | copy-start | bytes 14155780
  2.3 26.6 %collective-permute-start.2 = (f32[1752,128]{1,0:T(8,128)S(1)}, f32[1752,128]{1,0:T(8,128)S(1)}, u32[]{:S(2)}, u32[]{:S(2)}) collective-permute-start(f32[1752,128]{1,0:T(8,128)S(1)} %bitcast.13), channel_id=1, source_target_pairs={{0,1},{1,2},{2,3},{3,4},{4,5},{5,6},{6,7},{7,0},{8,9},{9,10},{10,1... | collective-permute-start | bytes 2691080 | tf_op jit(solution)/shard_map/ppermute | solution.py:354
  4.9 24.1 %collective-permute-start.3 = (f32[1752,128]{1,0:T(8,128)S(1)}, f32[1752,128]{1,0:T(8,128)S(1)}, u32[]{:S(2)}, u32[]{:S(2)}) collective-permute-start(f32[1752,128]{1,0:T(8,128)S(1)} %bitcast.11), channel_id=1, source_target_pairs={{0,7},{1,0},{2,1},{3,2},{4,3},{5,4},{6,5},{7,6},{8,15},{9,8},{10,9... | collective-permute-start | bytes 2691080 | tf_op jit(solution)/shard_map/ppermute | solution.py:355
  8.9 16.6 %copy-start.1 = (f32[1536]{0:T(1024)S(1)}, f32[1536]{0:T(1024)}, u32[]{:S(2)}) copy-start(f32[1536]{0:T(1024)} %param.3) | copy-start | bytes 18436
  10.5 13.0 %collective-permute-start.1 = (f32[576,128]{1,0:T(8,128)S(1)}, f32[576,128]{1,0:T(8,128)S(1)}, u32[]{:S(2)}, u32[]{:S(2)}) collective-permute-start(f32[576,128]{1,0:T(8,128)S(1)} %stage.1.after.z_edges), channel_id=1, source_target_pairs={{0,8},{8,16},{16,24},{24,0},{1,9},{9,17},{17,25},{25,1},{2,10},{10... | collective-permute-start | bytes 884744 | tf_op jit(solution)/shard_map/ppermute | solution.py:370
  11.8 14.5 %collective-permute-start = (f32[576,128]{1,0:T(8,128)S(1)}, f32[576,128]{1,0:T(8,128)S(1)}, u32[]{:S(2)}, u32[]{:S(2)}) collective-permute-start(f32[576,128]{1,0:T(8,128)S(1)} %stage.1.after.z_edges), channel_id=1, source_target_pairs={{0,24},{8,0},{16,8},{24,16},{1,25},{9,1},{17,9},{25,17},{2,26},{10... | collective-permute-start | bytes 884744 | tf_op jit(solution)/shard_map/ppermute | solution.py:369
  18.9 10.0 %collective-permute-start.4 = (f32[3,16,128]{2,1,0:T(8,128)S(1)}, f32[3,16,128]{2,1,0:T(8,128)S(1)}, u32[]{:S(2)}, u32[]{:S(2)}) collective-permute-start(f32[3,16,128]{2,1,0:T(8,128)S(1)} %get-tuple-element.23), channel_id=1, source_target_pairs={{0,32},{32,64},{64,96},{96,128},{128,160},{160,192},{192,224},{1,3... | collective-permute-start | bytes 73736 | tf_op jit(solution)/shard_map/ppermute | solution.py:382
  23.6 5.4 %collective-permute-start.5 = (f32[3,16,128]{2,1,0:T(8,128)S(1)}, f32[3,16,128]{2,1,0:T(8,128)S(1)}, u32[]{:S(2)}, u32[]{:S(2)}) collective-permute-start(f32[3,16,128]{2,1,0:T(8,128)S(1)} %get-tuple-element.20.after), channel_id=1, source_target_pairs={{32,0},{64,32},{96,64},{128,96},{160,128},{192,160},{224,192},{33,... | collective-permute-start | bytes 73736 | tf_op jit(solution)/shard_map/ppermute | solution.py:383
  31.4 1.9 %collective-permute-start.6 = (f32[2,48,128]{2,1,0:T(8,128)S(1)}, f32[2,48,128]{2,1,0:T(8,128)S(1)}, u32[]{:S(2)}, u32[]{:S(2)}) collective-permute-start(f32[2,48,128]{2,1,0:T(8,128)S(1)} %get-tuple-element.29.both), channel_id=1, source_target_pairs={{0,32},{32,0},{64,96},{96,64},{128,160},{160,128},{192,224},{224,1... | collective-permute-start | bytes 147464 | tf_op jit(solution)/shard_map/ppermute | solution.py:423
  33.3 6.8 %collective-permute-start.7 = (f32[48,128]{1,0:T(8,128)S(1)}, f32[48,128]{1,0:T(8,128)S(1)}, u32[]{:S(2)}, u32[]{:S(2)}) collective-permute-start(f32[48,128]{1,0:T(8,128)S(1)} %get-tuple-element.31), channel_id=1, source_target_pairs={{0,64},{32,96},{64,128},{96,160},{128,192},{160,224},{192,0},{224,... | collective-permute-start | bytes 73736 | tf_op jit(solution)/shard_map/ppermute | solution.py:442
  34.7 5.5 %collective-permute-start.8 = (f32[48,128]{1,0:T(8,128)S(1)}, f32[48,128]{1,0:T(8,128)S(1)}, u32[]{:S(2)}, u32[]{:S(2)}) collective-permute-start(f32[48,128]{1,0:T(8,128)S(1)} %get-tuple-element.32), channel_id=1, source_target_pairs={{0,128},{32,160},{64,192},{96,224},{128,0},{160,32},{192,64},{224,... | collective-permute-start | bytes 73736 | tf_op jit(solution)/shard_map/ppermute | solution.py:442
  37.3 2.9 %collective-permute-start.9 = (f32[48,128]{1,0:T(8,128)S(1)}, f32[48,128]{1,0:T(8,128)S(1)}, u32[]{:S(2)}, u32[]{:S(2)}) collective-permute-start(f32[48,128]{1,0:T(8,128)S(1)} %get-tuple-element.33), channel_id=1, source_target_pairs={{0,192},{32,224},{64,0},{96,32},{128,64},{160,96},{192,128},{224,1... | collective-permute-start | bytes 73736 | tf_op jit(solution)/shard_map/ppermute | solution.py:442
